TPU v7x, 128 devices: a whole 4x4x4 slice. The times are simulated.
128 devices in a mesh: ctx: 32 (over z, y_hi, x), seq: 4 (over y_lo, core).
Axes of the slice: x: 4, y: 4 (y_hi: 2, y_lo: 2; y = y_hi * 2 + y_lo), z: 4, core: 2. Of those that a mesh axis runs over, the one named last changes fastest.
Arguments:
- projected: bfloat16 [4, 3, 4096, 4096], P('seq', None, 'ctx'), may hold values from -6 to 6
- cotangent: bfloat16 [4, 4096, 4096], P('seq', 'ctx'), may hold values from -6 to 6
- short_filter: float32 [3, 7, 256], replicated, may hold values from -2.4 to 2.4
- residue: float32 [16, 256], replicated, may hold values from -0.09 to 0.09
- decay_rate: float32 [16, 256], replicated, may hold values from 7.927418e-06 to 0.3
Outputs:
- gated_output: bfloat16 [4, 4096, 4096], P('seq', 'ctx')
- grad_projected: bfloat16 [4, 3, 4096, 4096], P('seq', None, 'ctx')
- grad_short: float32 [3, 7, 256], replicated
- grad_residue: float32 [16, 256], replicated
- grad_log_decay: float32 [16, 256], replicated
All inputs are finite; a program needn't handle non-finite values.
Results may differ from a plain program's by a relative error of at most 0.001.
Values may be sent and summed in bfloat16 or wider, within the bound.
A program may use at most 192 MiB of HBM per device.

v0:
```python
from functools import partial
import math

import jax
import jax.numpy as jnp
from jax import lax
from jax.sharding import PartitionSpec as P

GROUP = 16


HIGHEST_PRECISION = lax.Precision.HIGHEST


def from_behind(block, axis, distance):
    devices = range(lax.axis_size(axis))
    route = [(i - distance, i) for i in devices if i - distance in devices]
    return lax.ppermute(block, axis, route)


def prefix(value, axis, join, neutral, backward):
    count, mine = (lax.axis_size(axis), lax.axis_index(axis))
    pieces = jax.tree.map(lambda part: lax.all_gather(part, axis), value)
    if backward:
        pieces = jax.tree.map(lambda part: part[::-1], pieces)
        mine = count - 1 - mine
    so_far = jax.tree.map(
        lambda part, zero: jnp.full_like(part, 0) + jnp.asarray(zero, part.dtype), value, neutral
    )

    def step(position, so_far):
        longer = join(so_far, jax.tree.map(lambda part: part[position], pieces))
        return jax.tree.map(lambda new, old: jnp.where(position < mine, new, old), longer, so_far)

    return lax.fori_loop(0, count - 1, step, so_far)


def featurize(padded, per_channel, row_count):
    reach_len = per_channel.shape[1] - 1
    summed = jnp.zeros((padded.shape[0], row_count, padded.shape[2]), jnp.float32)
    for tap_index in range(per_channel.shape[1]):
        window = padded[:, reach_len - tap_index : reach_len - tap_index + row_count, :]
        summed = summed + per_channel[:, tap_index, None, :] * window
    return summed


def transpose_featurize(extended, per_channel, row_count):
    summed = jnp.zeros((extended.shape[0], row_count, extended.shape[2]), jnp.float32)
    for tap_index in range(per_channel.shape[1]):
        summed = (
            summed
            + per_channel[:, tap_index, None, :] * extended[:, tap_index : tap_index + row_count, :]
        )
    return summed


def filter_terms(feat_grad, padded, row_count):
    reach_len = padded.shape[1] - row_count
    columns = []
    for tap_index in range(reach_len + 1):
        window = padded[:, reach_len - tap_index : reach_len - tap_index + row_count, :]
        columns.append(jnp.sum(feat_grad * window, axis=1))
    return jnp.stack(columns, axis=1)


def make_tables(residue, decay_rate, block_len):
    ramp_vec = jnp.arange(block_len, dtype=jnp.float32)
    rate_col = decay_rate[:, :, None]
    powers = jnp.exp(-rate_col * ramp_vec)
    inverse = jnp.exp(rate_col * ramp_vec)
    powers_next = jnp.exp(-rate_col * (ramp_vec + 1.0))
    tail_pow = jnp.exp(-rate_col * (block_len - 1.0 - ramp_vec))
    tail_lag = tail_pow * (block_len - 1.0 - ramp_vec)
    back_pow = jnp.exp(-rate_col * (block_len - ramp_vec))
    block_decay = jnp.exp(-decay_rate * block_len)[:, :, None]
    causal = (ramp_vec[:, None] >= ramp_vec[None, :]).astype(jnp.float32)
    toeplitz = (
        jnp.einsum(
            "mgi,mgj->gij", residue[:, :, None] * powers, inverse, precision=HIGHEST_PRECISION
        )
        * causal[None]
    )
    return (
        ramp_vec,
        powers,
        inverse,
        powers_next,
        tail_pow,
        tail_lag,
        back_pow,
        block_decay,
        causal,
        toeplitz,
    )


def block_forward(running, mixer_block, tables_all, residue):
    (
        ramp_vec,
        powers,
        inverse,
        powers_next,
        tail_pow,
        tail_lag,
        back_pow,
        block_decay,
        causal,
        toeplitz,
    ) = tables_all
    state_x, state_w = running
    block_len = mixer_block.shape[2]
    inside = jnp.einsum("gij,gcj->gci", toeplitz, mixer_block, precision=HIGHEST_PRECISION)
    carried = jnp.einsum(
        "mgi,mgc->gci", residue[:, :, None] * powers_next, state_x, precision=HIGHEST_PRECISION
    )
    next_x = block_decay * state_x + jnp.einsum(
        "mgj,gcj->mgc", tail_pow, mixer_block, precision=HIGHEST_PRECISION
    )
    next_w = block_decay * (state_w + block_len * state_x) + jnp.einsum(
        "mgj,gcj->mgc", tail_lag, mixer_block, precision=HIGHEST_PRECISION
    )
    return ((next_x, next_w), (inside + carried, state_x, state_w))


def block_backward(running, inputs_block, tables_all, residue):
    (
        ramp_vec,
        powers,
        inverse,
        powers_next,
        tail_pow,
        tail_lag,
        back_pow,
        block_decay,
        causal,
        toeplitz,
    ) = tables_all
    adjoint, grad_res, grad_lag = running
    conv_grad, mixer_block, start_x, start_w = inputs_block
    inside = jnp.einsum("gij,gci->gcj", toeplitz, conv_grad, precision=HIGHEST_PRECISION)
    carried = jnp.einsum(
        "mgj,mgc->gcj", residue[:, :, None] * back_pow, adjoint, precision=HIGHEST_PRECISION
    )
    next_adj = block_decay * adjoint + jnp.einsum(
        "mgi,gci->mgc", powers, conv_grad, precision=HIGHEST_PRECISION
    )
    pair_sums = (
        jnp.einsum("gci,gcj->gij", conv_grad, mixer_block, precision=HIGHEST_PRECISION)
        * causal[None]
    )
    inner_one = jnp.einsum("gij,mgj->gmi", pair_sums, inverse, precision=HIGHEST_PRECISION)
    inner_two = jnp.einsum(
        "gij,mgj->gmi", pair_sums, inverse * ramp_vec, precision=HIGHEST_PRECISION
    )
    local_res = jnp.einsum("gmi,mgi->mg", inner_one, powers, precision=HIGHEST_PRECISION)
    local_lag = jnp.einsum(
        "gmi,mgi->mg", inner_one * ramp_vec - inner_two, powers, precision=HIGHEST_PRECISION
    )
    meets_x = jnp.einsum("gci,mgc->mgi", conv_grad, start_x, precision=HIGHEST_PRECISION)
    meets_w = jnp.einsum("gci,mgc->mgi", conv_grad, start_w, precision=HIGHEST_PRECISION)
    cross_res = jnp.sum(powers_next * meets_x, axis=2)
    cross_lag = jnp.sum((ramp_vec + 1.0) * powers_next * meets_x + powers_next * meets_w, axis=2)
    return (
        (next_adj, grad_res + local_res + cross_res, grad_lag + local_lag + cross_lag),
        inside + carried,
    )


def to_blocks(rows_first, groups, block_count, block_len):
    return rows_first.T.reshape(groups, GROUP, block_count, block_len).transpose(2, 0, 1, 3)


def from_blocks(blocked, channels, row_count):
    return blocked.transpose(1, 2, 0, 3).reshape(channels, row_count)


def per_device(projected, cotangent, short_filter, residue, decay_rate):
    tokens = projected[0]
    upstream = cotangent[0]
    row_count = tokens.shape[1]
    channels = tokens.shape[2]
    groups = residue.shape[1]
    mode_count = residue.shape[0]
    reach_len = short_filter.shape[1] - 1
    block_len = math.gcd(row_count, 128)
    block_count = row_count // block_len
    per_channel = jnp.repeat(short_filter, GROUP, axis=2)
    decay_wide = jnp.repeat(decay_rate, GROUP, axis=1)
    before = from_behind(tokens[:, row_count - reach_len :, :], "ctx", 1)
    padded = jnp.concatenate([before, tokens], axis=1)
    features = featurize(padded, per_channel, row_count)
    mixer_in = features[1] * features[2]
    tables_all = make_tables(residue, decay_rate, block_len)
    mixer_blocks = to_blocks(mixer_in, groups, block_count, block_len)
    blank = jnp.zeros((mode_count, groups, GROUP), jnp.float32)
    (end_x, end_w), (conv_blocks, start_x, start_w) = lax.scan(
        partial(block_forward, tables_all=tables_all, residue=residue), (blank, blank), mixer_blocks
    )
    flat_blank = jnp.zeros((mode_count, channels), jnp.float32)
    length = jnp.asarray(float(row_count), jnp.float32)
    flat_x = end_x.reshape(mode_count, channels)
    flat_w = end_w.reshape(mode_count, channels)

    def join_forward(earlier, latter):
        factor = jnp.exp(-decay_wide * latter[2])
        return (
            factor * earlier[0] + latter[0],
            factor * (earlier[1] + latter[2] * earlier[0]) + latter[1],
            earlier[2] + latter[2],
        )

    into_x, into_w, unused_len = prefix(
        (flat_x, flat_w, length),
        "ctx",
        join_forward,
        (flat_blank, flat_blank, jnp.zeros((), jnp.float32)),
        False,
    )
    into_x3 = into_x.reshape(mode_count, groups, GROUP)
    into_w3 = into_w.reshape(mode_count, groups, GROUP)
    ramp_rows = jnp.arange(row_count, dtype=jnp.float32)
    conv_far = jnp.einsum(
        "mgt,mgc->gct",
        residue[:, :, None] * jnp.exp(-decay_rate[:, :, None] * (ramp_rows + 1.0)),
        into_x3,
        precision=HIGHEST_PRECISION,
    )
    long_conv = (
        from_blocks(conv_blocks, channels, row_count) + conv_far.reshape(channels, row_count)
    ).T
    offsets = jnp.arange(block_count, dtype=jnp.float32) * block_len
    offsets_col = offsets[:, None, None, None]
    factor_in = jnp.exp(-decay_rate[None, :, :, None] * offsets_col)
    true_x = start_x + factor_in * into_x3[None]
    true_w = start_w + factor_in * (into_w3[None] + offsets_col * into_x3[None])
    gated_output = (features[0] * long_conv).astype(jnp.bfloat16)
    conv_grad = upstream * features[0]
    first_grad = upstream * long_conv
    grad_zero = jnp.zeros((mode_count, groups), jnp.float32)
    grad_blocks = to_blocks(conv_grad, groups, block_count, block_len)
    (start_adj, grad_res, grad_lag), near_grad = lax.scan(
        partial(block_backward, tables_all=tables_all, residue=residue),
        (blank, grad_zero, grad_zero),
        (grad_blocks, mixer_blocks, true_x, true_w),
        reverse=True,
    )
    flat_adj = start_adj.reshape(mode_count, channels)

    def join_back(earlier, latter):
        factor = jnp.exp(-decay_wide * latter[1])
        return (factor * earlier[0] + latter[0], earlier[1] + latter[1])

    after_adj, unused_back = prefix(
        (flat_adj, length), "ctx", join_back, (flat_blank, jnp.zeros((), jnp.float32)), True
    )
    adj_far = jnp.einsum(
        "mgt,mgc->gct",
        residue[:, :, None] * jnp.exp(-decay_rate[:, :, None] * (row_count - ramp_rows)),
        after_adj.reshape(mode_count, groups, GROUP),
        precision=HIGHEST_PRECISION,
    )
    mixer_grad = (
        from_blocks(near_grad, channels, row_count) + adj_far.reshape(channels, row_count)
    ).T
    feat_grad = jnp.stack([first_grad, mixer_grad * features[2], mixer_grad * features[1]])
    following = from_behind(feat_grad[:, :reach_len, :], "ctx", -1)
    extended = jnp.concatenate([feat_grad, following], axis=1)
    grad_tokens = transpose_featurize(extended, per_channel, row_count).astype(jnp.bfloat16)
    short_terms = filter_terms(feat_grad, padded, row_count)
    taps_count = short_filter.shape[1]
    short_part = short_terms.reshape(3, taps_count, groups, GROUP).sum(axis=3)
    short_sum, res_sum, lag_sum = lax.psum((short_part, grad_res, grad_lag), ("ctx", "seq"))
    total_tokens = float(row_count * lax.axis_size("ctx") * lax.axis_size("seq"))
    grad_short = short_sum / total_tokens
    grad_residue = res_sum / total_tokens
    grad_log_decay = -residue * decay_rate * lag_sum / total_tokens
    return (gated_output[None], grad_tokens[None], grad_short, grad_residue, grad_log_decay)


def solution(mesh):
    placed = (P("seq", None, "ctx", None), P("seq", "ctx", None), P(), P(), P())
    return jax.shard_map(
        per_device,
        mesh=mesh,
        in_specs=placed,
        out_specs=(P("seq", "ctx", None), P("seq", None, "ctx", None), P(), P(), P()),
        check_vma=False,
    )
```

profile of v0, /device:TPU:1, one launch (start us, length us, event | category | flops | bytes accessed | tf_op | source)
XLA Modules:
  0.0 978.5 jit_solution(11184955967143783263)
XLA Ops:
  7.2 3.5 copy.114
  10.7 2.7 slice.114
  13.4 3.9 copy.115
  17.3 4.6 collective-permute-start
  21.9 2.0 broadcast_in_dim.30
  23.8 3.1 reshape.96
  27.9 2.3 copy.125
  36.4 3.6 copy.116
  40.0 26.9 %fusion.24 = f32[3,128,4096]{1,2,0:T(8,128)S(1)} fusion(bf16[3,128,4096]{1,2,0:T(8,128)(2,1)S(1)} %bitcast.135, f32[3,4096]{1,0:T(4,128)S(1)} %get-tuple-element.580, f32[3,4096]{1,0:T(4,128)} %get-tuple-element.581, f32[3,4096]{1,0:T(4,128)} %get-tuple-element.582, f32[3,4096]{1,0:T(4,128)} %get-tuple-element.583, f32[3,4096]{1,0:T(4,128)} %get-tuple-element.584, ...), kind=kLoop, calls=%fused_computation.51 | loop fusion | flops 59768832 | bytes 9928704 | tf_op jit(solution)/shard_map/add | solution.py:43
  68.5 3.6 bitcast_add_fusion.3
  75.0 82.1 %all-reduce = f32[32]{0:T(128)S(1)} all-reduce(f32[32]{0:T(128)S(1)} %dynamic-update-slice), channel_id=1, replica_groups=mesh['ctx'=32,'seq'=4] {'ctx'}, use_global_device_ids=true, to_apply=%add | all-reduce | flops 32 | bytes 256
  157.3 4.0 fusion.55
  161.3 30.4 %fusion.63 = f32[256,128,128]{2,1,0:T(8,128)} fusion(f32[16,256]{0,1:T(8,128)S(1)} %copy.119, f32[16,256]{0,1:T(8,128)S(1)} %copy.118, f32[16,256]{0,1:T(8,128)S(1)} %copy.117), kind=kOutput, calls=%fused_computation.118 | convolution fusion | flops 806879232 | bytes 16826368 | tf_op jit(solution)/shard_map/mgi,mgj->gij/dot_general | solution.py:78
  191.6 7.6 rev.7
  199.3 140.1 %while.24 = (s32[]{:T(128)}, f32[16,4096]{1,0:T(8,128)S(1)}, s32[]{:T(128)}, f32[32]{0:T(128)S(1)}, f32[32,16,4096]{2,1,0:T(8,128)}, /*index=5*/f32[16,256]{1,0:T(8,128)S(1)}, s32[]{:T(128)}, s32[]{:T(128)}) while((s32[]{:T(128)}, f32[16,4096]{1,0:T(8,128)S(1)}, s32[]{:T(128)}, f32[32]{0:T(128)S(1)}, f32[32,16,4096]{2,1,0:T(8,128)}, ...), condition=%wide.region_3.4_spmd.clone, body=%wide.region_2.3_spmd.clone.sunk | while | flops 327684 | bytes 1851525 | solution.py:35
  339.4 2.0 copy.153
  341.3 5.0 fusion.54
  346.4 16.8 %add_add_fusion = f32[256,16,128]{2,1,0:T(8,128)S(1)} fusion(f32[256,16,128]{2,1,0:T(8,128)S(1)} %fusion.54, f32[256,16,128]{2,1,0:T(8,128)S(1)} %copy-done.27, f32[256,16,128]{2,1,0:T(8,128)S(1)} %bitcast.130, f32[256,128,128]{2,1,0:T(8,128)} %fusion.63, f32[128,128]{1,0:T(8,128)S(1)} %fusion.101), kind=kOutput, calls=%fused_computation.105 | convolution fusion | flops 810549248 | bytes 25231360 | tf_op jit(solution)/shard_map/while/body/eval_jaxpr/gij,gci->gcj/dot_general | solution.py:140
  363.2 2.4 bitcast_multiply_fusion.4
  367.0 4.9 bitcast_add_fusion.5
  371.8 2.9 copy.122
  374.8 6.5 bitcast_add_fusion.4
  381.3 2.9 copy.123
  384.2 4.1 fusion.61
  388.3 26.8 %fusion.105 = f32[256,128,128]{2,1,0:T(8,128)S(1)} fusion(f32[256,16,128]{2,1,0:T(8,128)S(1)} %bitcast.131, f32[256,16,128]{2,1,0:T(8,128)S(1)} %bitcast.139), kind=kOutput, calls=%fused_computation.176 | convolution fusion | flops 805306368 | bytes 20971520 | tf_op jit(solution)/shard_map/while/body/eval_jaxpr/gci,gcj->gij/dot_general | solution.py:148
  415.1 26.8 %fusion.9 = f32[256,16,128]{2,1,0:T(8,128)S(1)} fusion(f32[256,128,128]{2,1,0:T(8,128)S(1)} %fusion.105, f32[128,128]{1,0:T(8,128)S(1)} %fusion.101, f32[16,256]{0,1:T(8,128)S(1)} %copy.119), kind=kOutput, calls=%fused_computation.11 | convolution fusion | flops 810024960 | bytes 18956288 | tf_op jit(solution)/shard_map/while/body/eval_jaxpr/gij,mgj->gmi/dot_general | solution.py:151
  443.3 28.0 %multiply_reduce_fusion = f32[16,256]{0,1:T(8,128)} fusion(f32[256,16,128]{2,1,0:T(8,128)S(1)} %fusion.9, f32[16,256]{0,1:T(8,128)S(1)} %copy.118, f32[256,128,128]{2,1,0:T(8,128)S(1)} %fusion.105, f32[128,128]{1,0:T(8,128)S(1)} %fusion.101, f32[16,256]{0,1:T(8,128)S(1)} %copy.119), kind=kOutput, calls=%fused_computation.99 | convolution fusion | flops 813166592 | bytes 18989056 | tf_op jit(solution)/shard_map/while/body/eval_jaxpr/gij,mgj->gmi/dot_general | solution.py:152
  471.3 15.5 %all-gather.4.cloned.1.call-done = f32[32,16,4096]{2,1,0:T(8,128)} async-done(((f32[1,16,4096]{2,1,0:T(8,128)}), f32[32,16,4096]{2,1,0:T(8,128)}) %all-gather.4.cloned.1.call-update) | async-done | bytes 8388624 | tf_op jit(solution)/shard_map/all_gather | solution.py:23
  486.8 105.0 %all-gather.6.cloned.1.call-done = f32[32,16,4096]{2,1,0:T(8,128)} async-done(((f32[1,16,4096]{2,1,0:T(8,128)}), f32[32,16,4096]{2,1,0:T(8,128)}) %all-gather.6.cloned.1.call-update) | async-done | bytes 8388624 | tf_op jit(solution)/shard_map/all_gather | solution.py:23
  591.8 146.4 %while.23 = (s32[]{:T(128)}, f32[16,4096]{1,0:T(8,128)S(1)}, f32[16,4096]{1,0:T(8,128)S(1)}, s32[]{:T(128)}, f32[32]{0:T(128)S(1)}, /*index=5*/f32[32,16,4096]{2...) while((s32[]{:T(128)}, f32[16,4096]{1,0:T(8,128)S(1)}, ...), condition=%wide.region_1.2_spmd.clone, body=%wide.region_0.1_spmd.clone.sunk | while | flops 720900 | bytes 2637973 | solution.py:35
  594.6 1.9 fusion.120
  739.0 5.5 fusion.50
  744.5 28.7 %add_add_fusion.1 = f32[256,16,128]{2,1,0:T(8,128)S(1)} fusion(f32[256,16,128]{2,1,0:T(8,128)S(1)} %fusion.50, f32[256,16,128]{2,1,0:T(8,128)S(1)} %copy-done.26, f32[256,16,128]{2,1,0:T(8,128)S(1)} %bitcast.140, f32[256,128,128]{2,1,0:T(8,128)} %fusion.63, f32[128,128]{1,0:T(8,128)S(1)} %copy-done.25), kind=kOutput, calls=%fused_computation.113 | convolution fusion | flops 810549248 | bytes 25231360 | tf_op jit(solution)/shard_map/while/body/eval_jaxpr/gij,gcj->gci/dot_general | solution.py:112
  773.3 3.3 fusion.45
  776.6 3.6 pad_maximum_fusion.1
  782.4 22.9 %fusion.30 = (f32[3,4096]{1,0:T(4,128)}, f32[3,4096]{1,0:T(4,128)}, f32[3,4096]{1,0:T(4,128)}, f32[3,4096]{1,0:T(4,128)S(1)}, f32[3,4096]{1,0:T(4,128)}, /*index=5*/f32[3,4096]{1,0:T(4,128)}, f32[3,4096]{1,0:T(4,128)}) fusion(bf16[3,128,4096]{1,2,0:T(8,128)(2,1)S(1)} %bitcast.136, bf16[3,6,4096]{1,2,0:T(8,128)(2,1)S(1)} %copy-done.16, ...), kind=kLoop, calls=%fused_computation.57 | loop fusion | flops 64401408 | bytes 13074432 | tf_op jit(solution)/shard_map/reduce_sum | solution.py:62
  806.6 5.2 copy.129
  828.7 2.0 broadcast_in_dim_reshape.2
  830.8 2.3 copy.136
  833.2 2.4 copy.132
  835.6 6.3 fusion.48
  841.9 2.4 copy.137
  844.4 5.2 fusion.47
  849.6 69.8 %all-reduce.1 = (f32[3,7,256]{2,0,1:T(4,128)S(1)}, f32[16,256]{0,1:T(8,128)S(1)}, f32[16,256]{0,1:T(8,128)S(1)}) all-reduce(f32[3,7,256]{2,0,1:T(4,128)S(1)} %copy-done.40, f32[16,256]{0,1:T(8,128)S(1)} %add.230, f32[16,256]{0,1:T(8,128)S(1)} %add.233), channel_id=1, replica_groups=mesh['ctx'=32,'seq'=4] {'ctx','seq'}, use_global_device_ids=true, to_apply=%region_12.13 | all-reduce | flops 13568 | bytes 108544 | tf_op jit(solution)/shard_map/psum | solution.py:272
  922.8 5.0 copy.130
  927.9 10.7 %pad_maximum_fusion = f32[3,134,4096]{1,2,0:T(8,128)} fusion(f32[3,6,4096]{1,2,0:T(8,128)} %copy.130, f32[1,128,4096]{1,2,0:T(8,128)} %bitcast.145, f32[1,128,4096]{1,2,0:T(8,128)S(1)} %bitcast.143, f32[1,128,4096]{1,2,0:T(8,128)} %copy-done.12), kind=kLoop, calls=%fused_computation.17 | loop fusion | flops 4939776 | bytes 13172736 | tf_op jit(solution)/shard_map/concatenate | solution.py:267
  938.6 28.3 %fusion.44 = bf16[1,3,128,4096]{2,3,1,0:T(8,128)(2,1)} fusion(f32[3,134,4096]{1,2,0:T(8,128)} %pad_maximum_fusion, f32[3,4096]{1,0:T(4,128)S(1)} %copy-done.33, f32[3,4096]{1,0:T(4,128)S(1)} %copy-done.34, f32[3,4096]{1,0:T(4,128)S(1)} %copy-done.35, f32[3,4096]{1,0:T(4,128)S(1)} %copy-done.36, f32[3,4096]{1,0:T(4,128)S(1)} %copy-done.37, ...), kind=kLoop, calls=%fused_computation.79 | loop fusion | flops 25165824 | bytes 47529984 | tf_op jit(solution)/shard_map/broadcast_in_dim | solution.py:277
  966.9 4.6 copy.139
  (408 shorter events, 322.3 us)
Async XLA Ops:
  7.2 184.5 %all-gather.8.cloned.1.call-start = ((), (), s32[]{:S(2)}) async-start(), calls=%async_computation.2 | async-start | bytes 8650752 | tf_op jit(solution)/shard_map/all_gather | solution.py:23
  10.7 29.3 %copy-start.3 = (bf16[1,3,128,4096]{2,3,1,0:T(8,128)(2,1)}, bf16[1,3,128,4096]{2,3,1,0:T(8,128)(2,1)S(1)}, u32[]{:S(2)}) copy-start(bf16[1,3,128,4096]{2,3,1,0:T(8,128)(2,1)S(1)} %copy.114) | copy-start | bytes 9437188
  13.4 8.5 copy-start.43
  17.3 19.1 %collective-permute-start = (bf16[3,6,4096]{2,1,0:T(8,128)(2,1)}, bf16[3,6,4096]{2,1,0:T(8,128)(2,1)}, u32[]{:S(2)}, u32[]{:S(2)}) collective-permute-start(bf16[3,6,4096]{2,1,0:T(8,128)(2,1)} %copy.115), channel_id=1, source_target_pairs={{0,4},{4,8},{8,12},{12,16},{16,20},{20,24},{24,28},{28,32},{32,36}... | collective-permute-start | bytes 442376 | tf_op jit(solution)/shard_map/ppermute | solution.py:18
  27.9 12.1 %copy-start.30 = (f32[3,1,4096]{2,0,1:T(4,128)}, f32[3,1,4096]{2,0,1:T(4,128)S(1)}, u32[]{:S(2)}) copy-start(f32[3,1,4096]{2,0,1:T(4,128)S(1)} %copy.180) | copy-start | bytes 147460
  31.7 35.1 %copy-start.32 = (f32[3,4096]{1,0:T(4,128)}, f32[3,4096]{1,0:T(4,128)S(1)}, u32[]{:S(2)}) copy-start(f32[3,4096]{1,0:T(4,128)S(1)} %get-tuple-element.580) | copy-start | bytes 147460
  40.0 26.9 %copy-start.17 = (bf16[1,128,4096]{1,2,0:T(8,128)(2,1)S(1)}, bf16[1,128,4096]{1,2,0:T(8,128)(2,1)}, u32[]{:S(2)}) copy-start(bf16[1,128,4096]{1,2,0:T(8,128)(2,1)} %copy.125) | copy-start | bytes 3145732
  66.9 5.2 copy-start.14
  68.5 5.0 copy-start.42
  68.5 5.1 copy-start.47
  68.5 88.6 %copy-start.44 = (f32[16,256]{1,0:T(8,128)S(1)}, f32[16,256]{1,0:T(8,128)}, u32[]{:S(2)}) copy-start(f32[16,256]{1,0:T(8,128)} %param.12) | copy-start | bytes 49156
  73.4 413.4 %all-gather.4.cloned.1.call-start = ((), (), s32[]{:S(2)}) async-start(), calls=%async_computation | async-start | bytes 8650752 | tf_op jit(solution)/shard_map/all_gather | solution.py:23
  73.6 368.4 %copy-start.19 = (f32[16,256]{0,1:T(8,128)}, f32[16,256]{0,1:T(8,128)S(1)}, u32[]{:S(2)}) copy-start(f32[16,256]{0,1:T(8,128)S(1)} %copy.119) | copy-start | bytes 49156
  157.2 581.7 %copy-start.21 = (f32[16,256]{0,1:T(8,128)}, f32[16,256]{0,1:T(8,128)S(1)}, u32[]{:S(2)}) copy-start(f32[16,256]{0,1:T(8,128)S(1)} %copy.117) | copy-start | bytes 49156
  157.3 284.7 %copy-start.24 = (f32[128,128]{1,0:T(8,128)}, f32[128,128]{1,0:T(8,128)S(1)}, u32[]{:S(2)}) copy-start(f32[128,128]{1,0:T(8,128)S(1)} %fusion.101) | copy-start | bytes 196612
  341.3 5.0 copy-start.1
  341.3 5.0 copy-start.27
  341.3 21.9 %slice-start = ((s8[6291456]{0:T(1024)(128)(4,1)}), s8[4194304]{0:T(1024)(128)(4,1)S(1)}, s32[]{:S(2)}) async-start(s8[6291456]{0:T(1024)(128)(4,1)} %bitcast.149), calls=%async_computation.3 | async-start | bytes 8388608
  346.4 16.8 %slice-start.1 = ((s8[6291456]{0:T(1024)(128)(4,1)}), s8[2097152]{0:T(1024)(128)(4,1)S(1)}, s32[]{:S(2)}) async-start(s8[6291456]{0:T(1024)(128)(4,1)} %bitcast.149), calls=%async_computation.4 | async-start | bytes 4194304
  374.7 217.1 %all-gather.6.cloned.1.call-start = ((), (), s32[]{:S(2)}) async-start(), calls=%async_computation.1 | async-start | bytes 8650752 | tf_op jit(solution)/shard_map/all_gather | solution.py:23
  384.2 354.7 %copy-start.45 = (f32[128]{0:T(128)}, f32[128]{0:T(128)S(1)}, u32[]{:S(2)}) copy-start(f32[128]{0:T(128)S(1)} %iota_add_fusion) | copy-start | bytes 1540
  738.9 5.6 copy-start.7
  739.0 5.6 copy-start.25
  739.0 5.6 copy-start.26
  744.5 28.7 %copy-start.18 = (bf16[1,128,4096]{1,2,0:T(8,128)(2,1)S(1)}, bf16[1,128,4096]{1,2,0:T(8,128)(2,1)}, u32[]{:S(2)}) copy-start(bf16[1,128,4096]{1,2,0:T(8,128)(2,1)} %copy.125) | copy-start | bytes 3145732
  776.6 4.3 copy-start.12
  776.6 4.2 copy-start.4
  776.6 5.9 copy-start.16
  811.8 111.0 %collective-permute-start.1 = (f32[3,6,4096]{2,1,0:T(8,128)}, f32[3,6,4096]{2,1,0:T(8,128)}, u32[]{:S(2)}, u32[]{:S(2)}) collective-permute-start(f32[3,6,4096]{2,1,0:T(8,128)} %copy.129), channel_id=1, source_target_pairs={{4,0},{8,4},{12,8},{16,12},{20,16},{24,20},{28,24},{32,28},{36,32}... | collective-permute-start | bytes 884744 | tf_op jit(solution)/shard_map/ppermute | solution.py:18
  828.7 4.4 copy-start.29
  828.7 4.4 copy-start.41
  830.8 4.8 copy-start.2
  830.8 4.8 copy-start.46
  844.3 5.2 copy-start.39
  844.3 5.3 copy-start.40
  844.3 75.1 %copy-start.23 = (bf16[128,4096]{0,1:T(8,128)(2,1)S(1)}, bf16[128,4096]{0,1:T(8,128)(2,1)}, u32[]{:S(2)}) copy-start(bf16[128,4096]{0,1:T(8,128)(2,1)} %get-tuple-element.566) | copy-start | bytes 3145732
  849.5 72.5 %copy-start.20 = (f32[16,256]{0,1:T(8,128)S(1)}, f32[16,256]{0,1:T(8,128)}, u32[]{:S(2)}) copy-start(f32[16,256]{0,1:T(8,128)} %copy-done.19) | copy-start | bytes 49156
  849.6 72.5 %copy-start.22 = (f32[16,256]{0,1:T(8,128)S(1)}, f32[16,256]{0,1:T(8,128)}, u32[]{:S(2)}) copy-start(f32[16,256]{0,1:T(8,128)} %copy-done.21) | copy-start | bytes 49156
  922.8 5.0 copy-start.9
  927.8 10.7 %copy-start.11 = (f32[128,4096]{0,1:T(8,128)S(1)}, f32[128,4096]{0,1:T(8,128)}, u32[]{:S(2)}) copy-start(f32[128,4096]{0,1:T(8,128)} %get-tuple-element.563) | copy-start | bytes 6291460
  927.8 10.7 %copy-start.13 = (f32[1,128,4096]{1,2,0:T(8,128)S(1)}, f32[1,128,4096]{1,2,0:T(8,128)}, u32[]{:S(2)}) copy-start(f32[1,128,4096]{1,2,0:T(8,128)} %copy-done.12) | copy-start | bytes 6291460
  927.8 10.7 %copy-start.31 = (f32[3,1,4096]{2,0,1:T(4,128)S(1)}, f32[3,1,4096]{2,0,1:T(4,128)}, u32[]{:S(2)}) copy-start(f32[3,1,4096]{2,0,1:T(4,128)} %copy-done.30) | copy-start | bytes 147460
  927.8 10.7 %copy-start.33 = (f32[3,4096]{1,0:T(4,128)S(1)}, f32[3,4096]{1,0:T(4,128)}, u32[]{:S(2)}) copy-start(f32[3,4096]{1,0:T(4,128)} %copy-done.32) | copy-start | bytes 147460
  927.8 10.7 %copy-start.34 = (f32[3,4096]{1,0:T(4,128)S(1)}, f32[3,4096]{1,0:T(4,128)}, u32[]{:S(2)}) copy-start(f32[3,4096]{1,0:T(4,128)} %get-tuple-element.581) | copy-start | bytes 147460
  927.8 10.7 %copy-start.35 = (f32[3,4096]{1,0:T(4,128)S(1)}, f32[3,4096]{1,0:T(4,128)}, u32[]{:S(2)}) copy-start(f32[3,4096]{1,0:T(4,128)} %get-tuple-element.582) | copy-start | bytes 147460
  927.8 10.7 %copy-start.36 = (f32[3,4096]{1,0:T(4,128)S(1)}, f32[3,4096]{1,0:T(4,128)}, u32[]{:S(2)}) copy-start(f32[3,4096]{1,0:T(4,128)} %get-tuple-element.583) | copy-start | bytes 147460
  927.8 10.7 %copy-start.37 = (f32[3,4096]{1,0:T(4,128)S(1)}, f32[3,4096]{1,0:T(4,128)}, u32[]{:S(2)}) copy-start(f32[3,4096]{1,0:T(4,128)} %get-tuple-element.584) | copy-start | bytes 147460
  927.9 10.7 %copy-start.38 = (f32[3,4096]{1,0:T(4,128)S(1)}, f32[3,4096]{1,0:T(4,128)}, u32[]{:S(2)}) copy-start(f32[3,4096]{1,0:T(4,128)} %get-tuple-element.585) | copy-start | bytes 147460
  (7 other events, 19.0 us)
Sparse Core Ops, SparseCore 0:
  73.5 106.5 all-gather.7
  374.8 111.8 all-gather.3
  489.8 101.9 all-gather.5
where the time goes:
time: 989 us; the launch traced here: 979 us
  local copies, waits for them, and re-layouts  267 us (27%)
  other arithmetic  214 us (22%)
  matrix products  202 us (20%)
  blocking collectives  152 us (15%)
  waiting for transfers between devices  121 us (12%)
  between operations  15 us (2%)
    all_gather x3, waiting for transfers between devices, prefix(): pieces = jax.tree.map(lambda part: lax.all_gather(part, axis), value)  121 us
    select_n x62, other arithmetic, step(): jnp.where(position < mine, new, old)  113 us
    neg x62, local copies, waits for them, and re-layouts, join_forward(): factor = jnp.exp(-decay_wide * latter[2])  96.5 us
    unnamed x1, blocking collectives  82.1 us
    psum x1, blocking collectives, per_device(): lax.psum((short_part, grad_res, grad_lag), ('ctx', 'seq'))  69.8 us
    dynamic_slice x62, local copies, waits for them, and re-layouts, step(): longer = join(so_far, jax.tree.map(lambda part: part[position], pieces))  39 us
    broadcast_in_dim x62, local copies, waits for them, and re-layouts, per_device(): decay_wide = jnp.repeat(decay_rate, GROUP, axis=1)  37 us
    unnamed x122, local copies, waits for them, and re-layouts  30.5 us
  transfers between devices with their start and end apart: 5, of which 2 were waited for; matrix products, arithmetic and copies ran while one was open for 19% of the time, Pallas kernels for 0%

commit v1 on v0

v1 whole, which is shorter than its diff:
```python
from functools import partial

import jax
import jax.numpy as jnp
from jax import lax
from jax.experimental import pallas as pl
from jax.experimental.pallas import tpu as pltpu
from jax.sharding import PartitionSpec as P

GROUP = 16
MODES = 16
TAPS = 7
LANES = 128
TILE_GROUPS = LANES // GROUP
ROWS = 128
F32, BF16 = jnp.float32, jnp.bfloat16
MESH = pl.DeviceIdType.MESH

DECAY, RESIDUE, SHORT, DECAY_GM, RESIDUE_GM, TABLE_ROWS = 0, 16, 32, 53, 54, 56


def split(value):
    high = value.astype(BF16)
    return high, (value - high.astype(F32)).astype(BF16)


def iota(shape, dim):
    return lax.broadcasted_iota(jnp.int32, shape, dim)


def dot(left, right):
    return jnp.dot(left, right, preferred_element_type=F32)


def in_group(rows, width, group):
    return (iota((rows, width), 1) % LANES) // GROUP == group


def flip_matrix():
    return (iota((ROWS, ROWS), 0) + iota((ROWS, ROWS), 1) == ROWS - 1).astype(BF16)


def load_tokens(pad, proj_ref, before_ref, lanes):
    for i in range(3):
        pad[i, 0:8, :] = before_ref[i, :, lanes]
        pad[i, 8 : 8 + ROWS, :] = proj_ref[i, :, lanes].astype(F32)


def feature(pad, taps, i, start, count):
    total = None
    for j in range(TAPS):
        term = taps[TAPS * i + j] * pad[i, 8 + start - j : 8 + start - j + count, :]
        total = term if total is None else total + term
    return total


def tap_rows(wide_ref, lanes):
    return [wide_ref[SHORT + k : SHORT + k + 1, lanes] for k in range(3 * TAPS)]


def halo_kernel(
    n, proj_ref, cot_ref, before_ref, after_ref, rows_tail, rows_head, out_f, out_b, got_f, got_b,
    load_sem, send_sem, recv_sem,
):
    me = lax.axis_index("ctx")
    right, left = lax.rem(me + 1, n), lax.rem(me + n - 1, n)
    loads = [
        pltpu.make_async_copy(proj_ref.at[:, pl.ds(ROWS - 16, 16), :], rows_tail, load_sem.at[0]),
        pltpu.make_async_copy(
            proj_ref.at[:, pl.ds(0, 16), :], rows_head.at[pl.ds(0, 3)], load_sem.at[1]
        ),
        pltpu.make_async_copy(cot_ref.at[pl.ds(0, 16), :], rows_head.at[3], load_sem.at[2]),
    ]
    for load in loads:
        load.start()
    barrier = pltpu.get_barrier_semaphore()
    for neighbour in (left, right):
        pl.semaphore_signal(barrier, inc=1, device_id={"ctx": neighbour}, device_id_type=MESH)
    for load in loads:
        load.wait()
    half = rows_tail.shape[2] // 2
    for i in range(3):
        tail = rows_tail[i].astype(F32)[8:16]
        out_f[i] = jnp.concatenate([tail[:, :half], tail[:, half:]], axis=0).astype(BF16)
    for i in range(4):
        head = rows_head[i].astype(F32)[0:8]
        out_b[i] = jnp.concatenate([head[:, :half], head[:, half:]], axis=0).astype(BF16)
    pl.semaphore_wait(barrier, 2)
    copies = [
        pltpu.make_async_remote_copy(
            src_ref=source,
            dst_ref=target,
            send_sem=send_sem.at[k],
            recv_sem=recv_sem.at[k],
            device_id={"ctx": to},
            device_id_type=MESH,
        )
        for k, (source, target, to) in enumerate([(out_f, got_f, right), (out_b, got_b, left)])
    ]
    for copy in copies:
        copy.start()
    for copy in copies:
        copy.wait()
    first, last = me == 0, me == n - 1
    for i in range(3):
        part = jnp.where(first, 0.0, got_f[i].astype(F32))
        before_ref[i, :, 0:half] = part[0:8]
        before_ref[i, :, half : 2 * half] = part[8:16]
    for i in range(4):
        part = jnp.where(last, 0.0, got_b[i].astype(F32))
        after_ref[i, :, 0:half] = part[0:8]
        after_ref[i, :, half : 2 * half] = part[8:16]


def exchange_halo(n, tokens, cotangent):
    channels = tokens.shape[2]
    half = channels // 2
    return pl.pallas_call(
        partial(halo_kernel, n),
        out_shape=[
            jax.ShapeDtypeStruct((3, 8, channels), F32),
            jax.ShapeDtypeStruct((4, 8, channels), F32),
        ],
        in_specs=[pl.BlockSpec(memory_space=pl.ANY)] * 2,
        out_specs=[pl.BlockSpec(memory_space=pltpu.VMEM)] * 2,
        scratch_shapes=[
            pltpu.VMEM((3, 16, channels), BF16),
            pltpu.VMEM((4, 16, channels), BF16),
            pltpu.VMEM((3, 16, half), BF16),
            pltpu.VMEM((4, 16, half), BF16),
            pltpu.VMEM((3, 16, half), BF16),
            pltpu.VMEM((4, 16, half), BF16),
            pltpu.SemaphoreType.DMA((3,)),
            pltpu.SemaphoreType.DMA((2,)),
            pltpu.SemaphoreType.DMA((2,)),
        ],
        compiler_params=pltpu.CompilerParams(
            collective_id=0, has_side_effects=True, vmem_limit_bytes=32 * 2**20
        ),
        name="halo",
    )(tokens, cotangent)


def local_kernel(
    tiles, proj_ref, cot_ref, before_ref, wide_ref, ends_ref, local_ref, feat_ref, near_ref,
    pad, parts, left, right, left_pair, right_pair,
):
    def one_tile(tile, carry):
        lanes = pl.ds(pl.multiple_of(tile * LANES, LANES), LANES)
        load_tokens(pad, proj_ref, before_ref, lanes)
        taps = tap_rows(wide_ref, lanes)
        step = 32
        for start in range(0, ROWS, step):
            rows = slice(start, start + step)
            f = [feature(pad, taps, i, start, step) for i in range(3)]
            for i in range(3):
                feat_ref[i, rows, lanes] = f[i]
            high, low = split(f[1] * f[2])
            right[rows, 0:LANES] = high
            right[ROWS + start : ROWS + start + step, 0:LANES] = high
            right[2 * ROWS + start : 2 * ROWS + start + step, 0:LANES] = low
            right_pair[rows, 0:LANES] = high
            right_pair[rows, LANES : 2 * LANES] = high
            right_pair[ROWS + start : ROWS + start + step, 0:LANES] = low
            right_pair[ROWS + start : ROWS + start + step, LANES : 2 * LANES] = low
            high, low = split(cot_ref[rows, lanes].astype(F32) * f[0])
            parts[rows, 0:LANES] = high
            parts[rows, LANES : 2 * LANES] = low
        flipped = dot(flip_matrix(), parts[...]).astype(BF16)
        right[0:ROWS, LANES : 2 * LANES] = flipped[:, 0:LANES]
        right[ROWS : 2 * ROWS, LANES : 2 * LANES] = flipped[:, 0:LANES]
        right[2 * ROWS : 3 * ROWS, LANES : 2 * LANES] = flipped[:, LANES : 2 * LANES]

        decay = wide_ref[DECAY : DECAY + MODES, lanes]
        residue = wide_ref[RESIDUE : RESIDUE + MODES, lanes]
        back = (LANES - 1 - iota((MODES, LANES), 1)).astype(F32)
        powers = []
        for g in range(TILE_GROUPS):
            column = GROUP * g
            power = jnp.exp(-decay[:, column : column + 1] * back)
            powers.append(power)
            filter_row = jnp.sum(residue[:, column : column + 1] * power, axis=0, keepdims=True)
            base = pltpu.roll(
                jnp.broadcast_to(filter_row, (8, LANES)), 1, 1, stride=1, stride_axis=0
            )
            for q in range(0, ROWS, 16):
                block = jnp.concatenate(
                    [pltpu.roll(base, q, 1) if q else base, pltpu.roll(base, q + 8, 1)], axis=0
                )
                keep = iota((16, LANES), 1) <= iota((16, LANES), 0) + q
                high, low = split(jnp.where(keep, block, 0.0))
                at = slice(ROWS * g + q, ROWS * g + q + 16)
                left[at, 0:LANES] = high
                left[at, LANES : 2 * LANES] = low
                left[at, 2 * LANES : 3 * LANES] = high
            for k, value in enumerate((power, back * power)):
                high, low = split(value)
                begin = TILE_GROUPS * (ROWS + k * MODES) + MODES * g
                at = slice(begin, begin + MODES)
                left[at, 0:LANES] = high
                left[at, LANES : 2 * LANES] = low
                left[at, 2 * LANES : 3 * LANES] = high
            left_pair[ROWS * g : ROWS * (g + 1), :] = jnp.where(
                in_group(ROWS, 2 * LANES, g), flipped, jnp.zeros_like(flipped)
            )
        product = dot(left[...], right[...])

        def gather(begin, count):
            total = product[begin : begin + count]
            for g in range(1, TILE_GROUPS):
                at = begin + g * count
                total = jnp.where(in_group(count, 2 * LANES, g), product[at : at + count], total)
            return total

        near = gather(0, ROWS)
        near_ref[0, :, lanes] = near[:, 0:LANES]
        near_ref[1, :, lanes] = near[:, LANES : 2 * LANES]
        ends = gather(TILE_GROUPS * ROWS, MODES)
        ends_ref[tile, 0:MODES, :] = ends[:, 0:LANES]
        ends_ref[tile, MODES : 2 * MODES, :] = ends[:, LANES : 2 * LANES]
        lags = gather(TILE_GROUPS * (ROWS + MODES), MODES)
        local_ref[tile, 0:MODES, :] = lags[:, 0:LANES]
        local_ref[tile, MODES : 2 * MODES, :] = lags[:, LANES : 2 * LANES]

        pairs = lax.dot_general(
            left_pair[...], right_pair[...], (((1,), (1,)), ((), ())), preferred_element_type=F32
        )
        res_sum = jnp.zeros((MODES, LANES), F32)
        lag_sum = jnp.zeros((MODES, LANES), F32)
        lane = iota((MODES, LANES), 1)
        for g in range(TILE_GROUPS):
            total = None
            for q in range(0, ROWS, 8):
                at = slice(ROWS * g + q, ROWS * g + q + 8)
                block = pairs[at, 0:LANES] + pairs[at, LANES : 2 * LANES]
                keep = iota((8, LANES), 1) + iota((8, LANES), 0) <= ROWS - 1 - q
                block = jnp.where(keep, block, 0.0)
                if q:
                    block = pltpu.roll(block, q, 1)
                total = block if total is None else total + block
            by_lag = jnp.sum(
                pltpu.roll(total, 0, 1, stride=1, stride_axis=0), axis=0, keepdims=True
            )
            weighted = powers[g] * by_lag
            res_sum = jnp.where(
                lane == GROUP * g, jnp.sum(weighted, axis=1, keepdims=True), res_sum
            )
            lag_sum = jnp.where(
                lane == GROUP * g, jnp.sum(back * weighted, axis=1, keepdims=True), lag_sum
            )
        local_ref[tile, 2 * MODES : 3 * MODES, :] = res_sum
        local_ref[tile, 3 * MODES : 4 * MODES, :] = lag_sum
        return carry

    lax.fori_loop(0, tiles, one_tile, 0)


def local_part(tokens, cotangent, before, wide, block):
    channels = tokens.shape[2]
    tiles = block // LANES
    count = channels // LANES
    return pl.pallas_call(
        partial(local_kernel, tiles),
        grid=(channels // block,),
        in_specs=[
            pl.BlockSpec((3, ROWS, block), lambda t: (0, 0, t)),
            pl.BlockSpec((ROWS, block), lambda t: (0, t)),
            pl.BlockSpec((3, 8, block), lambda t: (0, 0, t)),
            pl.BlockSpec((TABLE_ROWS, block), lambda t: (0, t)),
        ],
        out_specs=[
            pl.BlockSpec((tiles, 2 * MODES, LANES), lambda t: (t, 0, 0)),
            pl.BlockSpec((tiles, 4 * MODES, LANES), lambda t: (t, 0, 0)),
            pl.BlockSpec((3, ROWS, block), lambda t: (0, 0, t)),
            pl.BlockSpec((2, ROWS, block), lambda t: (0, 0, t)),
        ],
        out_shape=[
            jax.ShapeDtypeStruct((count, 2 * MODES, LANES), F32),
            jax.ShapeDtypeStruct((count, 4 * MODES, LANES), F32),
            jax.ShapeDtypeStruct((3, ROWS, channels), F32),
            jax.ShapeDtypeStruct((2, ROWS, channels), F32),
        ],
        scratch_shapes=[
            pltpu.VMEM((3, ROWS + 8, LANES), F32),
            pltpu.VMEM((ROWS, 2 * LANES), BF16),
            pltpu.VMEM((TILE_GROUPS * (ROWS + 2 * MODES), 3 * LANES), BF16),
            pltpu.VMEM((3 * ROWS, 2 * LANES), BF16),
            pltpu.VMEM((TILE_GROUPS * ROWS, 2 * LANES), BF16),
            pltpu.VMEM((2 * ROWS, 2 * LANES), BF16),
        ],
        compiler_params=pltpu.CompilerParams(vmem_limit_bytes=48 * 2**20),
        name="local",
    )(tokens, cotangent, before, wide)


def state_kernel(n, ends_ref, decay_ref, into_ref, cross_ref, got, back, s_out, r_out, s_in, r_in):
    me = lax.axis_index("ctx")

    def peer_of(k):
        return lax.rem(me + k, n)

    barrier = pltpu.get_barrier_semaphore()

    def greet(k, carry):
        pl.semaphore_signal(barrier, inc=1, device_id={"ctx": peer_of(k)}, device_id_type=MESH)
        return carry

    lax.fori_loop(1, n, greet, 0)
    got[me] = ends_ref[me]
    decay = decay_ref[me]
    pl.semaphore_wait(barrier, n - 1)

    def send_out(k):
        return pltpu.make_async_remote_copy(
            src_ref=ends_ref.at[peer_of(k)],
            dst_ref=got.at[me],
            send_sem=s_out.at[k],
            recv_sem=r_out.at[me],
            device_id={"ctx": peer_of(k)},
            device_id_type=MESH,
        )

    def receive_out(k):
        source = lax.rem(me + n - k, n)
        return pltpu.make_async_remote_copy(
            src_ref=ends_ref.at[source],
            dst_ref=got.at[source],
            send_sem=s_out.at[k],
            recv_sem=r_out.at[source],
            device_id={"ctx": source},
            device_id_type=MESH,
        )

    def send_in(k):
        return pltpu.make_async_remote_copy(
            src_ref=back.at[peer_of(k)],
            dst_ref=into_ref.at[me],
            send_sem=s_in.at[k],
            recv_sem=r_in.at[me],
            device_id={"ctx": peer_of(k)},
            device_id_type=MESH,
        )

    def receive_in(k):
        source = lax.rem(me + n - k, n)
        return pltpu.make_async_remote_copy(
            src_ref=back.at[source],
            dst_ref=into_ref.at[source],
            send_sem=s_in.at[k],
            recv_sem=r_in.at[source],
            device_id={"ctx": source},
            device_id_type=MESH,
        )

    def each(action):
        def run(k, carry):
            action(k)
            return carry

        lax.fori_loop(1, n, run, 0)

    each(lambda k: send_out(k).start())
    each(lambda k: receive_out(k).wait_recv())
    pole = jnp.exp(-decay)
    whole = jnp.exp(-decay * float(ROWS))
    zero = jnp.zeros((MODES, LANES), F32)

    def forward(d, carry):
        state, lagged, res, lag = carry
        adjoint = got[d, MODES : 2 * MODES, :]
        back[d, 0:MODES, :] = state
        res = res + adjoint * state
        lag = lag + adjoint * (state + float(ROWS) * lagged)
        return whole * state + got[d, 0:MODES, :], whole * (lagged + state), res, lag

    _, _, res, lag = lax.fori_loop(0, n, forward, (zero, zero, zero, zero))
    cross_ref[0] = pole * res
    cross_ref[1] = pole * lag

    def backward(k, state):
        d = n - 1 - k
        back[d, MODES : 2 * MODES, :] = state
        return whole * state + got[d, MODES : 2 * MODES, :]

    lax.fori_loop(0, n, backward, zero)
    each(lambda k: send_in(k).start())
    into_ref[me] = back[me]
    each(lambda k: receive_in(k).wait_recv())
    each(lambda k: send_out(k).wait_send())
    each(lambda k: send_in(k).wait_send())


def exchange_states(n, ends, decay_tiles):
    vmem = pl.BlockSpec(memory_space=pltpu.VMEM)
    return pl.pallas_call(
        partial(state_kernel, n),
        out_shape=[
            jax.ShapeDtypeStruct((n, 2 * MODES, LANES), F32),
            jax.ShapeDtypeStruct((2, MODES, LANES), F32),
        ],
        in_specs=[vmem, vmem],
        out_specs=[vmem, vmem],
        scratch_shapes=[
            pltpu.VMEM((n, 2 * MODES, LANES), F32),
            pltpu.VMEM((n, 2 * MODES, LANES), F32),
        ]
        + [pltpu.SemaphoreType.DMA((n,))] * 4,
        compiler_params=pltpu.CompilerParams(
            collective_id=1, has_side_effects=True, vmem_limit_bytes=16 * 2**20
        ),
        name="states",
    )(ends, decay_tiles)


def finish_kernel(
    tiles, me_ref, proj_ref, cot_ref, before_ref, after_ref, wide_ref, ends_ref, local_ref,
    feat_ref, near_ref, into_ref, cross_ref, gated_ref, grad_ref, sums_ref,
    pad, grads, left, right, flip_parts,
):
    step_index = pl.program_id(0)

    def one_tile(tile, carry):
        lanes = pl.ds(pl.multiple_of(tile * LANES, LANES), LANES)
        load_tokens(pad, proj_ref, before_ref, lanes)
        for i in range(3):
            pad[i, 8 + ROWS : 16 + ROWS, :] = after_ref[i, :, lanes]
        taps = tap_rows(wide_ref, lanes)
        decay = wide_ref[DECAY : DECAY + MODES, lanes]
        residue = wide_ref[RESIDUE : RESIDUE + MODES, lanes]
        decay_row = wide_ref[DECAY_GM : DECAY_GM + 1, lanes]
        residue_row = wide_ref[RESIDUE_GM : RESIDUE_GM + 1, lanes]

        ahead = (iota((ROWS, LANES), 0) + 1).astype(F32)
        high, low = split(residue_row * jnp.exp(-decay_row * ahead))
        left[:, 0:LANES] = high
        left[:, LANES : 2 * LANES] = low
        left[:, 2 * LANES : 3 * LANES] = high
        state = into_ref[tile, 0:MODES, :]
        adjoint = into_ref[tile, MODES : 2 * MODES, :]
        high, low = split(jnp.concatenate([state, adjoint], axis=1))
        for g in range(TILE_GROUPS):
            keep = in_group(MODES, 2 * LANES, g)
            chosen = jnp.where(keep, high, jnp.zeros_like(high))
            right[MODES * g : MODES * (g + 1), :] = chosen
            right[ROWS + MODES * g : ROWS + MODES * (g + 1), :] = chosen
            right[2 * ROWS + MODES * g : 2 * ROWS + MODES * (g + 1), :] = jnp.where(
                keep, low, jnp.zeros_like(low)
            )
        far = dot(left[...], right[...])
        long_conv = near_ref[0, :, lanes] + far[:, 0:LANES]
        high, low = split(near_ref[1, :, lanes] + far[:, LANES : 2 * LANES])
        flip_parts[0:ROWS, :] = high
        flip_parts[ROWS : 2 * ROWS, :] = low
        flip = flip_matrix()
        mixer_grad = dot(jnp.concatenate([flip, flip], axis=1), flip_parts[...])

        gated_ref[:, lanes] = (feat_ref[0, :, lanes] * long_conv).astype(BF16)
        grads[0, 0:ROWS, :] = cot_ref[:, lanes].astype(F32) * long_conv
        grads[1, 0:ROWS, :] = mixer_grad * feat_ref[2, :, lanes]
        grads[2, 0:ROWS, :] = mixer_grad * feat_ref[1, :, lanes]

        pole = jnp.exp(-decay)
        inverse = jnp.exp(decay)
        next_feat = [feature(pad, taps, i, ROWS, 8) for i in range(3)]
        next_cot = after_ref[3, :, lanes]
        next_in = next_feat[1] * next_feat[2]
        next_grad = next_cot * next_feat[0]
        whole = jnp.exp(-decay * float(ROWS))
        behind = residue * pole * (whole * state + ends_ref[tile, 0:MODES, :])
        beyond = residue * adjoint
        lag_pos = residue
        lag_neg = residue * inverse
        conv_rows, mixer_rows, filters, filters_neg = [], [], [], []
        for k in range(TAPS - 1):
            filters.append(jnp.sum(lag_pos, axis=0, keepdims=True))
            filters_neg.append(jnp.sum(lag_neg, axis=0, keepdims=True))
            conv = jnp.sum(behind, axis=0, keepdims=True)
            mixer = jnp.sum(beyond, axis=0, keepdims=True)
            for j in range(k + 1):
                conv = conv + filters[k - j] * next_in[j : j + 1]
            for j in range(k):
                mixer = mixer - filters_neg[k - j - 1] * next_grad[j : j + 1]
            conv_rows.append(conv)
            mixer_rows.append(mixer)
            lag_pos, lag_neg = lag_pos * pole, lag_neg * inverse
            behind, beyond = behind * pole, beyond * inverse
        blank = jnp.zeros((8 - (TAPS - 1), LANES), F32)
        next_conv = jnp.concatenate(conv_rows + [blank], axis=0)
        next_mixer = jnp.concatenate(mixer_rows + [blank], axis=0)
        grads[0, ROWS : ROWS + 8, :] = next_cot * next_conv
        grads[1, ROWS : ROWS + 8, :] = next_mixer * next_feat[2]
        grads[2, ROWS : ROWS + 8, :] = next_mixer * next_feat[1]

        step = 32
        short = []
        for i in range(3):
            sums = [None] * TAPS
            for start in range(0, ROWS, step):
                rows = slice(start, start + step)
                own = grads[i, rows, :]
                total = None
                for j in range(TAPS):
                    ahead_grad = grads[i, start + j : start + j + step, :]
                    term = taps[TAPS * i + j] * ahead_grad
                    total = term if total is None else total + term
                    product = own * pad[i, 8 + start - j : 8 + start - j + step, :]
                    part = product[0:8]
                    for r in range(8, step, 8):
                        part = part + product[r : r + 8]
                    sums[j] = part if sums[j] is None else sums[j] + part
                grad_ref[i, rows, lanes] = total.astype(BF16)
            short += [jnp.sum(part, axis=0, keepdims=True) for part in sums]
        short.append(jnp.zeros((3, LANES), F32))

        mine = step_index * tiles + tile == me_ref[0]
        res_sum = local_ref[tile, 2 * MODES : 3 * MODES, :]
        lag_sum = local_ref[tile, 3 * MODES : 4 * MODES, :]
        lag_sum = lag_sum + pole * (
            local_ref[tile, MODES : 2 * MODES, :] * state + local_ref[tile, 0:MODES, :] * adjoint
        )
        res_sum = res_sum + jnp.where(mine, cross_ref[0], 0.0)
        lag_sum = lag_sum + jnp.where(mine, cross_ref[1], 0.0)
        high, low = split(jnp.concatenate(short + [res_sum, lag_sum], axis=0))
        member = (iota((2 * LANES, LANES), 0) % LANES) // GROUP == iota((2 * LANES, LANES), 1)
        by_group = dot(
            jnp.concatenate([high, low], axis=1), member.astype(F32).astype(BF16)
        )
        packed = by_group[0:8]
        for r in range(8, TABLE_ROWS, 8):
            packed = packed + pltpu.roll(by_group[r : r + 8], r, 1)
        sums_ref[tile] = packed
        return carry

    lax.fori_loop(0, tiles, one_tile, 0)


def finish(me, tokens, cotangent, before, after, wide, ends, local, feats, near, into, cross, block):
    channels = tokens.shape[2]
    tiles = block // LANES
    count = channels // LANES

    def per_tile(rows):
        return pl.BlockSpec((tiles, rows, LANES), lambda t: (t, 0, 0))

    def stack(k, rows):
        return pl.BlockSpec((k, rows, block), lambda t: (0, 0, t))

    plane = pl.BlockSpec((ROWS, block), lambda t: (0, t))
    return pl.pallas_call(
        partial(finish_kernel, tiles),
        grid=(channels // block,),
        in_specs=[
            pl.BlockSpec(memory_space=pltpu.SMEM),
            stack(3, ROWS),
            plane,
            stack(3, 8),
            stack(4, 8),
            pl.BlockSpec((TABLE_ROWS, block), lambda t: (0, t)),
            per_tile(2 * MODES),
            per_tile(4 * MODES),
            stack(3, ROWS),
            stack(2, ROWS),
            per_tile(2 * MODES),
            pl.BlockSpec((2, MODES, LANES), lambda t: (0, 0, 0)),
        ],
        out_specs=[plane, stack(3, ROWS), per_tile(8)],
        out_shape=[
            jax.ShapeDtypeStruct((ROWS, channels), BF16),
            jax.ShapeDtypeStruct((3, ROWS, channels), BF16),
            jax.ShapeDtypeStruct((count, 8, LANES), F32),
        ],
        scratch_shapes=[
            pltpu.VMEM((3, ROWS + 16, LANES), F32),
            pltpu.VMEM((3, ROWS + 8, LANES), F32),
            pltpu.VMEM((ROWS, 3 * LANES), BF16),
            pltpu.VMEM((3 * ROWS, 2 * LANES), BF16),
            pltpu.VMEM((2 * ROWS, LANES), BF16),
        ],
        compiler_params=pltpu.CompilerParams(vmem_limit_bytes=48 * 2**20),
        name="finish",
    )(me, tokens, cotangent, before, after, wide, ends, local, feats, near, into, cross)


def total_kernel(n, m, part_ref, out_ref, got, rows, s_a, r_a, s_b, r_b, s_c, r_c):
    me, mine = lax.axis_index("ctx"), lax.axis_index("seq")
    barrier = pltpu.get_barrier_semaphore()

    def each(count, action):
        def run(k, carry):
            action(k)
            return carry

        lax.fori_loop(1, count, run, 0)

    def copy(axis, source, target, send_sem, recv_sem, to):
        return pltpu.make_async_remote_copy(
            src_ref=source,
            dst_ref=target,
            send_sem=send_sem,
            recv_sem=recv_sem,
            device_id={axis: to},
            device_id_type=MESH,
        )

    def to_ctx(k):
        return lax.rem(me + k, n)

    def from_ctx(k):
        return lax.rem(me + n - k, n)

    def to_seq(k):
        return lax.rem(mine + k, m)

    def from_seq(k):
        return lax.rem(mine + m - k, m)

    def greet(axis, to):
        pl.semaphore_signal(barrier, inc=1, device_id={axis: to}, device_id_type=MESH)

    each(n, lambda k: greet("ctx", to_ctx(k)))
    each(m, lambda k: greet("seq", to_seq(k)))
    got[me] = part_ref[me]
    pl.semaphore_wait(barrier, n - 1 + m - 1)

    def first(k, to, slot):
        return copy("ctx", part_ref.at[to], got.at[slot], s_a.at[k], r_a.at[slot], to)

    each(n, lambda k: first(k, to_ctx(k), me).start())
    each(n, lambda k: first(k, from_ctx(k), from_ctx(k)).wait_recv())
    total = got[0]
    for d in range(1, n):
        total = total + got[d]
    rows[mine] = total

    def second(k, to, slot):
        return copy("seq", rows.at[mine], rows.at[slot], s_b.at[k], r_b.at[slot], to)

    each(m, lambda k: second(k, to_seq(k), mine).start())
    each(m, lambda k: second(k, from_seq(k), from_seq(k)).wait_recv())
    total = rows[0]
    for d in range(1, m):
        total = total + rows[d]
    out_ref[me] = total

    def third(k, to, slot):
        return copy("ctx", out_ref.at[me], out_ref.at[slot], s_c.at[k], r_c.at[slot], to)

    each(n, lambda k: third(k, to_ctx(k), me).start())
    each(n, lambda k: third(k, from_ctx(k), from_ctx(k)).wait_recv())
    each(n, lambda k: first(k, to_ctx(k), me).wait_send())
    each(m, lambda k: second(k, to_seq(k), mine).wait_send())
    each(n, lambda k: third(k, to_ctx(k), me).wait_send())


def total_sums(n, m, parts):
    vmem = pl.BlockSpec(memory_space=pltpu.VMEM)
    return pl.pallas_call(
        partial(total_kernel, n, m),
        out_shape=jax.ShapeDtypeStruct((n, 8, LANES), F32),
        in_specs=[vmem],
        out_specs=vmem,
        scratch_shapes=[pltpu.VMEM((n, 8, LANES), F32), pltpu.VMEM((m, 8, LANES), F32)]
        + [pltpu.SemaphoreType.DMA((n,))] * 2
        + [pltpu.SemaphoreType.DMA((m,))] * 2
        + [pltpu.SemaphoreType.DMA((n,))] * 2,
        compiler_params=pltpu.CompilerParams(
            collective_id=2, has_side_effects=True, vmem_limit_bytes=16 * 2**20
        ),
        name="totals",
    )(parts)


def per_device(projected, cotangent, short_filter, residue, decay_rate):
    n, m = lax.axis_size("ctx"), lax.axis_size("seq")
    tokens, upstream = projected[0], cotangent[0]
    channels = tokens.shape[2]
    groups = residue.shape[1]
    block = min(channels, 512)
    by_group = jnp.concatenate([decay_rate, residue, short_filter.reshape(3 * TAPS, groups)])
    wide = jnp.concatenate(
        [
            jnp.repeat(by_group, GROUP, axis=1),
            decay_rate.T.reshape(1, channels),
            residue.T.reshape(1, channels),
            jnp.zeros((1, channels), F32),
        ]
    )
    decay_tiles = wide[0:MODES].reshape(MODES, n, LANES).transpose(1, 0, 2)
    me = lax.axis_index("ctx").astype(jnp.int32).reshape(1)

    before, after = exchange_halo(n, tokens, upstream)
    ends, local, feats, near = local_part(tokens, upstream, before, wide, block)
    into, cross = exchange_states(n, ends, decay_tiles)
    gated, grad_tokens, sums = finish(
        me, tokens, upstream, before, after, wide, ends, local, feats, near, into, cross, block
    )
    sums = total_sums(n, m, sums)
    blocks = TABLE_ROWS // 8
    sums = sums[:, :, 0 : blocks * TILE_GROUPS].reshape(n, 8, blocks, TILE_GROUPS)
    sums = sums.transpose(2, 1, 0, 3).reshape(TABLE_ROWS, groups)
    sums = sums / float(ROWS * n * m)
    grad_short = sums[0 : 3 * TAPS].reshape(3, TAPS, groups)
    grad_residue = sums[24 : 24 + MODES]
    grad_log_decay = -residue * decay_rate * sums[40 : 40 + MODES]
    return gated[None], grad_tokens[None], grad_short, grad_residue, grad_log_decay


def solution(mesh):
    placed = (P("seq", None, "ctx", None), P("seq", "ctx", None), P(), P(), P())
    return jax.shard_map(
        per_device,
        mesh=mesh,
        in_specs=placed,
        out_specs=(P("seq", "ctx", None), P("seq", None, "ctx", None), P(), P(), P()),
        check_vma=False,
    )
```

time: 989 us -> 154 us (0.16)
  local copies, waits for them, and re-layouts: 267 us -> 14.6 us
  other arithmetic: 214 us -> 2.76 us
  matrix products: 202 us -> 0 us
  blocking collectives: 152 us -> 0 us
  Pallas kernels: 0 us -> 135 us
  waiting for transfers between devices: 121 us -> 0 us
  between operations: 15 us -> 0.81 us
    dot_general x15 -> x0, matrix products: 202 us -> none  [the longest x1 30.4 us: make_tables(): jnp.einsum('mgi,mgj->gij', residue[:, :, None] * powers, inverse, precisi...]
    pallas_call x0 -> x5, Pallas kernels: none -> 135 us  [the longest x1 44.4 us: local_part(): pl.pallas_call(partial(local_kernel, tiles), grid=(channels // block,), i...]
    all_gather x3 -> x0, waiting for transfers between devices: 121 us -> none  [prefix(): pieces = jax.tree.map(lambda part: lax.all_gather(part, axis), value)]
    select_n x62 -> x0, other arithmetic: 113 us -> none  [step(): jnp.where(position < mine, new, old)]
    neg x63 -> x0, local copies, waits for them, and re-layouts: 96.6 us -> none  [the longest x62 96.5 us: join_forward(): factor = jnp.exp(-decay_wide * latter[2])]
    unnamed x1 -> x0, blocking collectives: 82.1 us -> none
    psum x1 -> x0, blocking collectives: 69.8 us -> none  [per_device(): lax.psum((short_part, grad_res, grad_lag), ('ctx', 'seq'))]
    dynamic_slice x62 -> x0, local copies, waits for them, and re-layouts: 39 us -> none  [step(): longer = join(so_far, jax.tree.map(lambda part: part[position], pieces))]
  transfers between devices with their start and end apart: 5 -> 0, of which waited for: 2 -> 0; matrix products, arithmetic and copies ran while one was open for 19% -> 0% of each run, Pallas kernels for 0% -> 0%
where the time goes in v1:
time: 154 us; the launch traced here: 153 us
  Pallas kernels  135 us (88%)
  local copies, waits for them, and re-layouts  14.6 us (9%)
  other arithmetic  2.76 us (2%)
    pallas_call x1, Pallas kernels, local_part(): pl.pallas_call(partial(local_kernel, tiles), grid=(channels // block,), i...  44.4 us
    pallas_call x1, Pallas kernels, finish(): pl.pallas_call(partial(finish_kernel, tiles), grid=(channels // block,),...  27.4 us
    pallas_call x1, Pallas kernels, exchange_states(): pl.pallas_call(partial(state_kernel, n), out_shape=[jax.ShapeDtypeStruct(...  24.6 us
    pallas_call x1, Pallas kernels, total_sums(): pl.pallas_call(partial(total_kernel, n, m), out_shape=jax.ShapeDtypeStruc...  23.9 us
    pallas_call x1, Pallas kernels, exchange_halo(): pl.pallas_call(partial(halo_kernel, n), out_shape=[jax.ShapeDtypeStruct((...  14.8 us
    unnamed x10, local copies, waits for them, and re-layouts  3.13 us

profile of v1, /device:TPU:1, one launch (start us, length us, event | category | flops | bytes accessed | tf_op | source)
XLA Modules:
  0.0 153.3 jit_solution(11767223762625797628)
XLA Ops:
  0.6 0.1 pad.3.clone
  0.7 0.7 reshape.42
  1.5 0.7 pad_maximum_fusion
  2.2 0.1 copy.14
  2.3 0.8 copy.15
  3.1 0.1 reshape.44
  3.2 0.8 copy.16
  4.1 0.1 reshape.45
  4.2 0.0 copy-start
  4.2 1.9 %copy-done = bf16[1,3,128,4096]{3,2,1,0:T(8,128)(2,1)S(1)} copy-done((bf16[1,3,128,4096]{3,2,1,0:T(8,128)(2,1)S(1)}, bf16[1,3,128,4096]{3,2,1,0:T(8,128)(2,1)}, u32[]{:S(2)}) %copy-start) | copy-done | bytes 3145752
  6.1 0.0 copy-start.1
  6.1 1.2 copy-done.1
  7.3 14.8 %halo.1 = (f32[3,8,4096]{2,1,0:T(8,128)S(1)}, f32[4,8,4096]{2,1,0:T(8,128)S(1)}) custom-call(bf16[3,128,4096]{2,1,0:T(8,128)(2,1)S(1)} %bitcast.23, bf16[128,4096]{1,0:T(8,128)(2,1)S(1)} %bitcast.24), custom_call_target="tpu_custom_call" | custom-call | tf_op jit(solution)/shard_map/halo/pallas_call | solution.py:118
  22.1 0.0 copy-start.3
  22.1 0.1 broadcast_in_dim.14
  22.3 1.6 %copy.17 = f32[53,4096]{1,0:T(8,128)} copy(f32[53,4096]{0,1:T(8,128)S(1)} %bitcast.28) | data formatting | bytes 1736704 | tf_op jit(solution)/shard_map/reshape | solution.py:682
  23.8 0.0 copy-start.2
  23.8 1.4 maximum_maximum_fusion.wide_ref
  25.2 0.0 copy-done.3
  25.2 1.9 %broadcast_in_dim.16 = f32[16,256,16]{2,1,0:T(8,128)} broadcast(f32[16,256]{1,0:T(8,128)S(1)} %copy-done.3), dimensions={0,1} | broadcast | bytes 278528 | tf_op jit(solution)/shard_map/broadcast_in_dim | solution.py:682
  27.2 2.2 %reshape.46 = f32[16,32,128]{2,1,0:T(8,128)S(1)} reshape(f32[16,256,16]{2,1,0:T(8,128)} %broadcast_in_dim.16) | data formatting | bytes 524288 | tf_op jit(solution)/shard_map/reshape | solution.py:688
  29.3 0.2 copy.24
  29.5 0.0 copy-done.2
  29.5 44.4 %local.1 = (f32[32,32,128]{2,1,0:T(8,128)S(1)}, f32[32,64,128]{2,1,0:T(8,128)S(1)}, f32[3,128,4096]{2,1,0:T(8,128)}, f32[2,128,4096]{2,1,0:T(8,128)}) custom-call(bf16[3,128,4096]{2,1,0:T(8,128)(2,1)} %bitcast.21, bf16[128,4096]{1,0:T(8,128)(2,1)S(1)} %bitcast.25, f32[3,8,4096]{2,1,0:T(8,128)S(1)} %get-tuple-element.16.before_ref, ...), custom_call_target="tpu_custom_call" | custom-call | tf_op jit(solution)/shard_map/local/pallas_call | solution.py:262
  73.9 24.6 %states.1 = (f32[32,32,128]{2,1,0:T(8,128)S(1)}, f32[2,16,128]{2,1,0:T(8,128)S(1)}) custom-call(f32[32,32,128]{2,1,0:T(8,128)S(1)} %get-tuple-element.18.ends_ref, f32[32,16,128]{2,1,0:T(8,128)S(1)} %bitcast.27), custom_call_target="tpu_custom_call" | custom-call | tf_op jit(solution)/shard_map/states/pallas_call | solution.py:395
  98.6 0.0 copy-start.4
  98.6 27.4 %finish.1 = (bf16[128,4096]{1,0:T(8,128)(2,1)}, bf16[3,128,4096]{2,1,0:T(8,128)(2,1)}, f32[32,8,128]{2,1,0:T(8,128)S(1)}) custom-call(s32[1]{0:T(128)} %bitcast.me_ref, bf16[3,128,4096]{2,1,0:T(8,128)(2,1)} %bitcast.22, bf16[128,4096]{1,0:T(8,128)(2,1)S(1)} %bitcast.26, f32[3,8,4096]{2,1,0:T(8,128)S(1)} %get-tuple-element.16.before_ref, ...), custom_call_target="tpu_custom_call" | custom-call | tf_op jit(solution)/shard_map/finish/pallas_call | solution.py:549
  126.0 23.9 %totals.1 = f32[32,8,128]{2,1,0:T(8,128)S(1)} custom-call(f32[32,8,128]{2,1,0:T(8,128)S(1)} %get-tuple-element.26.part_ref), custom_call_target="tpu_custom_call" | custom-call | tf_op jit(solution)/shard_map/totals/pallas_call | solution.py:657
  149.9 0.1 copy.19
  150.1 0.1 copy.22
  150.2 0.2 slice.26
  150.4 0.0 copy-done.4
  150.4 0.6 multiply_multiply_fusion
  151.0 0.1 copy.21
  151.1 0.8 slice.24
  151.9 0.3 copy.20
  152.2 0.5 div.16
  152.7 0.6 reshape.47
  (3 shorter events, 0.0 us)
Async XLA Ops:
  4.2 1.9 %copy-start = (bf16[1,3,128,4096]{3,2,1,0:T(8,128)(2,1)S(1)}, bf16[1,3,128,4096]{3,2,1,0:T(8,128)(2,1)}, u32[]{:S(2)}) copy-start(bf16[1,3,128,4096]{3,2,1,0:T(8,128)(2,1)} %param.5) | copy-start | bytes 9437188
  6.1 1.2 copy-start.1
  22.1 3.1 %copy-start.3 = (f32[16,256]{1,0:T(8,128)S(1)}, f32[16,256]{1,0:T(8,128)}, u32[]{:S(2)}) copy-start(f32[16,256]{1,0:T(8,128)} %param.9) | copy-start | bytes 49156
  23.8 5.7 %copy-start.2 = (bf16[1,128,4096]{2,1,0:T(8,128)(2,1)S(1)}, bf16[1,128,4096]{2,1,0:T(8,128)(2,1)}, u32[]{:S(2)}) copy-start(bf16[1,128,4096]{2,1,0:T(8,128)(2,1)} %param.6) | copy-start | bytes 3145732
  98.6 51.8 %copy-start.4 = (f32[16,256]{1,0:T(8,128)S(1)}, f32[16,256]{1,0:T(8,128)}, u32[]{:S(2)}) copy-start(f32[16,256]{1,0:T(8,128)} %param.8) | copy-start | bytes 49156

commit v2 on v0

v2 whole, which is shorter than its diff:
```python
from functools import partial

import jax
import jax.numpy as jnp
from jax import lax
from jax.experimental import pallas as pl
from jax.experimental.pallas import tpu as pltpu
from jax.sharding import PartitionSpec as P

GROUP = 16
MODES = 16
TAPS = 7
LANES = 128
TILE_GROUPS = LANES // GROUP
ROWS = 128
F32, BF16 = jnp.float32, jnp.bfloat16
MESH = pl.DeviceIdType.MESH

HALF = ROWS // 2
WAYS = 2

DECAY, RESIDUE, SHORT, TABLE_ROWS = 0, 16, 32, 56


def split(value):
    high = value.astype(BF16)
    return high, (value - high.astype(F32)).astype(BF16)


def iota(shape, dim):
    return lax.broadcasted_iota(jnp.int32, shape, dim)


def dot(left, right):
    return jnp.dot(left, right, preferred_element_type=F32)


def in_group(rows, width, group):
    return (iota((rows, width), 1) % LANES) // GROUP == group


def flip_matrix():
    return (iota((ROWS, ROWS), 0) + iota((ROWS, ROWS), 1) == ROWS - 1).astype(BF16)


def load_tokens(pad, proj_ref, before_ref, lanes):
    for i in range(3):
        pad[i, 0:8, :] = before_ref[i, :, lanes]
        pad[i, 8 : 8 + ROWS, :] = proj_ref[i, :, lanes].astype(F32)


def feature(pad, taps, i, start, count):
    total = None
    for j in range(TAPS):
        term = taps[TAPS * i + j] * pad[i, 8 + start - j : 8 + start - j + count, :]
        total = term if total is None else total + term
    return total


def tap_rows(wide_ref, lanes):
    return [wide_ref[SHORT + k : SHORT + k + 1, lanes] for k in range(3 * TAPS)]


def expand_table(wide_ref, small, decay_ref, residue_ref, short_ref):
    small[DECAY : DECAY + MODES, :] = decay_ref[...]
    small[RESIDUE : RESIDUE + MODES, :] = residue_ref[...]
    for i in range(3):
        small[SHORT + TAPS * i : SHORT + TAPS * (i + 1), :] = short_ref[i]
    used = SHORT + 3 * TAPS
    groups = small.shape[1]
    small[used:TABLE_ROWS, :] = jnp.zeros((TABLE_ROWS - used, groups), F32)
    value = small[...]
    high = value.astype(BF16).astype(F32)
    middle = (value - high).astype(BF16).astype(F32)
    low = value - high - middle
    pieces = jnp.concatenate([high, middle, low], axis=0).astype(BF16)
    width = min(1024, wide_ref.shape[1])
    for start in range(0, wide_ref.shape[1], width):
        owner = (iota((groups, width), 1) + start) // GROUP
        spread = (iota((groups, width), 0) == owner).astype(F32).astype(BF16)
        got = dot(pieces, spread)
        wide_ref[:, start : start + width] = got[0:TABLE_ROWS] + (
            got[TABLE_ROWS : 2 * TABLE_ROWS] + got[2 * TABLE_ROWS :]
        )


def lanes_of(tile):
    return pl.ds(pl.multiple_of(tile * LANES, LANES), LANES)


def select_groups(source, begin, count, rows, columns):
    total = source[begin + rows.start : begin + rows.stop, columns]
    for g in range(1, TILE_GROUPS):
        at = begin + g * count
        total = jnp.where(
            in_group(rows.stop - rows.start, columns.stop - columns.start, g),
            source[at + rows.start : at + rows.stop, columns],
            total,
        )
    return total


def local_kernel(
    n, proj_ref, cot_ref, decay_ref, residue_ref, short_ref,
    wide_ref, before_ref, after_ref, ends_ref, local_ref, near_ref, into_ref,
    small, out_f, out_b, got_f, got_b, got, back, tables, rights, pad, parts, *scratch,
):
    products, left_pairs, right_pairs, pair_sums = (
        scratch[k * WAYS : (k + 1) * WAYS] for k in range(4)
    )
    halo_send, halo_recv, s_out, r_out, s_in, r_in = scratch[4 * WAYS :]
    me = lax.axis_index("ctx")
    right_dev, left_dev = lax.rem(me + 1, n), lax.rem(me + n - 1, n)
    far_back = (LANES - 1 - iota((MODES, LANES), 1)).astype(F32)

    def peer_of(k):
        return lax.rem(me + k, n)

    def each(action):
        def run(k, carry):
            action(k)
            return carry

        lax.fori_loop(1, n, run, 0)

    def remote(source, target, send_sem, recv_sem, to):
        return pltpu.make_async_remote_copy(
            src_ref=source,
            dst_ref=target,
            send_sem=send_sem,
            recv_sem=recv_sem,
            device_id={"ctx": to},
            device_id_type=MESH,
        )

    barrier = pltpu.get_barrier_semaphore()
    each(
        lambda k: pl.semaphore_signal(
            barrier, inc=1, device_id={"ctx": peer_of(k)}, device_id_type=MESH
        )
    )
    width = out_f.shape[2]
    for i in range(3):
        tail = proj_ref[i, ROWS - 16 : ROWS, :].astype(F32)[8:16]
        out_f[i] = jnp.concatenate([tail[:, :width], tail[:, width:]], axis=0).astype(BF16)
    for i in range(4):
        head = (cot_ref[0:16, :] if i == 3 else proj_ref[i, 0:16, :]).astype(F32)[0:8]
        out_b[i] = jnp.concatenate([head[:, :width], head[:, width:]], axis=0).astype(BF16)
    expand_table(wide_ref, small, decay_ref, residue_ref, short_ref)
    pl.semaphore_wait(barrier, n - 1)
    halo = [
        remote(out_f, got_f, halo_send.at[0], halo_recv.at[0], right_dev),
        remote(out_b, got_b, halo_send.at[1], halo_recv.at[1], left_dev),
    ]
    for copy in halo:
        copy.start()

    def power_of(tile, g):
        column = GROUP * g
        decay = wide_ref[DECAY : DECAY + MODES, lanes_of(tile)]
        return jnp.exp(-decay[:, column : column + 1] * far_back)

    def store_table(tile, at, value):
        high, low = split(value)
        tables[tile, at, 0:LANES] = high
        tables[tile, at, LANES : 2 * LANES] = low
        tables[tile, at, 2 * LANES : 3 * LANES] = high

    def build_tables(tile, carry):
        residue = wide_ref[RESIDUE : RESIDUE + MODES, lanes_of(tile)]
        for g in range(TILE_GROUPS):
            column = GROUP * g
            power = power_of(tile, g)
            filter_row = jnp.sum(residue[:, column : column + 1] * power, axis=0, keepdims=True)
            base = pltpu.roll(
                jnp.broadcast_to(filter_row, (8, LANES)), 1, 1, stride=1, stride_axis=0
            )
            for q in range(HALF, ROWS, 16):
                block = jnp.concatenate(
                    [pltpu.roll(base, q, 1), pltpu.roll(base, q + 8, 1)], axis=0
                )
                keep = iota((16, LANES), 1) <= iota((16, LANES), 0) + q
                begin = HALF * g + q - HALF
                store_table(tile, slice(begin, begin + 16), jnp.where(keep, block, 0.0))
            for k, value in enumerate((power, far_back * power)):
                begin = TILE_GROUPS * (HALF + k * MODES) + MODES * g
                store_table(tile, slice(begin, begin + MODES), value)
        return carry

    lax.fori_loop(0, n, build_tables, 0)

    for copy in halo:
        copy.wait()
    first, last = me == 0, me == n - 1
    for i in range(3):
        part = jnp.where(first, 0.0, got_f[i].astype(F32))
        before_ref[i, :, 0:width] = part[0:8]
        before_ref[i, :, width : 2 * width] = part[8:16]
    for i in range(4):
        part = jnp.where(last, 0.0, got_b[i].astype(F32))
        after_ref[i, :, 0:width] = part[0:8]
        after_ref[i, :, width : 2 * width] = part[8:16]

    def features(tile, way):
        lanes = lanes_of(tile)
        load_tokens(pad, proj_ref, before_ref, lanes)
        taps = tap_rows(wide_ref, lanes)
        step = 32
        for start in range(0, ROWS, step):
            rows = slice(start, start + step)
            f = [feature(pad, taps, i, start, step) for i in range(3)]
            high, low = split(f[1] * f[2])
            for k, value in enumerate((high, high, low)):
                begin = ROWS * k + start
                rights[tile, begin : begin + step, 0:LANES] = value
                if start < HALF:
                    begin = begin + HALF
                    rights[tile, begin : begin + step, 2 * LANES : 3 * LANES] = value
            high, low = split(cot_ref[rows, lanes].astype(F32) * f[0])
            begin = 2 * LANES * way
            parts[rows, begin : begin + LANES] = high
            parts[rows, begin + LANES : begin + 2 * LANES] = low

    def place(tile, flipped):
        blank = jnp.zeros((HALF, 2 * LANES), BF16)
        for k, column in enumerate((0, 0, LANES)):
            value = flipped[:, column : column + LANES]
            begin = ROWS * k
            rights[tile, begin : begin + ROWS, LANES : 2 * LANES] = value
            rights[tile, begin : begin + HALF, 2 * LANES : 4 * LANES] = blank
            rights[tile, begin + HALF : begin + ROWS, 3 * LANES : 4 * LANES] = value[0:HALF]

    modes, both = slice(0, MODES), slice(0, 2 * LANES)

    def send_out(k):
        return remote(
            ends_ref.at[peer_of(k)], got.at[me], s_out.at[k], r_out.at[me], peer_of(k)
        )

    group = 4 if n % 4 == 0 else 2

    def begin_tiles(step, carry):
        ks = [step * group + way for way in range(group)]
        for way, k in enumerate(ks):
            features(peer_of(k), way)
        flipped = dot(flip_matrix(), parts[:, 0 : 2 * LANES * group]).astype(BF16)
        for way, k in enumerate(ks):
            place(peer_of(k), flipped[:, 2 * LANES * way : 2 * LANES * (way + 1)])
        states = [
            dot(tables[peer_of(k), TILE_GROUPS * HALF :, :], rights[peer_of(k), :, both])
            for k in ks
        ]
        for k, state in zip(ks, states):
            tile = peer_of(k)
            ends = select_groups(state, 0, MODES, modes, both)
            ends_ref[tile, 0:MODES, :] = ends[:, 0:LANES]
            ends_ref[tile, MODES : 2 * MODES, :] = ends[:, LANES : 2 * LANES]
            lags = select_groups(state, TILE_GROUPS * MODES, MODES, modes, both)
            local_ref[tile, 0:MODES, :] = lags[:, 0:LANES]
            local_ref[tile, MODES : 2 * MODES, :] = lags[:, LANES : 2 * LANES]
        for k in ks:

            @pl.when(k != 0)
            def _():
                send_out(k).start()

        return carry

    lax.fori_loop(0, n // group, begin_tiles, 0)

    def convolve(step, carry):
        tiles = [step * WAYS + way for way in range(WAYS)]
        for way, tile in enumerate(tiles):
            products[way][...] = dot(tables[tile, 0 : TILE_GROUPS * HALF, :], rights[tile])
        for way, tile in enumerate(tiles):
            for start in range(0, ROWS, 32):
                source = start % HALF
                columns = slice(0, 2 * LANES) if start >= HALF else slice(2 * LANES, 4 * LANES)
                near = select_groups(
                    products[way], 0, HALF, slice(source, source + 32), columns
                )
                near_ref[0, start : start + 32, lanes_of(tile)] = near[:, 0:LANES]
                near_ref[1, start : start + 32, lanes_of(tile)] = near[:, LANES : 2 * LANES]
        return carry

    lax.fori_loop(0, n // WAYS, convolve, 0)

    def receive_out(k):
        source = lax.rem(me + n - k, n)
        return remote(ends_ref.at[source], got.at[source], s_out.at[k], r_out.at[source], source)

    def send_in(k):
        return remote(back.at[peer_of(k)], into_ref.at[me], s_in.at[k], r_in.at[me], peer_of(k))

    def receive_in(k):
        source = lax.rem(me + n - k, n)
        return remote(back.at[source], into_ref.at[source], s_in.at[k], r_in.at[source], source)

    got[me] = ends_ref[me]
    each(lambda k: receive_out(k).wait_recv())
    decay = wide_ref[DECAY : DECAY + MODES, lanes_of(me)]
    pole = jnp.exp(-decay)
    whole = jnp.exp(-decay * float(ROWS))
    zero = jnp.zeros((MODES, LANES), F32)

    def scan(step, carry):
        state, lagged, res, lag, beyond = carry
        for k in range(2):
            d = step * 2 + k
            adjoint = got[d, MODES : 2 * MODES, :]
            back[d, 0:MODES, :] = state
            res = res + adjoint * state
            lag = lag + adjoint * (state + float(ROWS) * lagged)
            state, lagged = whole * state + got[d, 0:MODES, :], whole * (lagged + state)
            d = n - 1 - d
            back[d, MODES : 2 * MODES, :] = beyond
            beyond = whole * beyond + got[d, MODES : 2 * MODES, :]
        return state, lagged, res, lag, beyond

    _, _, cross_res, cross_lag, _ = lax.fori_loop(0, n // 2, scan, (zero,) * 5)
    each(lambda k: send_in(k).start())
    into_ref[me] = back[me]

    lane = iota((MODES, LANES), 1)

    def correlate(step, carry):
        tiles = [step * WAYS + way for way in range(WAYS)]
        for way, tile in enumerate(tiles):
            flipped = jnp.concatenate(
                [
                    rights[tile, 0:ROWS, LANES : 2 * LANES],
                    rights[tile, 2 * ROWS : 3 * ROWS, LANES : 2 * LANES],
                ],
                axis=1,
            )
            for g in range(TILE_GROUPS):
                left_pairs[way][ROWS * g : ROWS * (g + 1), :] = jnp.where(
                    in_group(ROWS, 2 * LANES, g), flipped, jnp.zeros_like(flipped)
                )
            for k in range(2):
                value = rights[tile, 2 * ROWS * k : 2 * ROWS * k + ROWS, 0:LANES]
                right_pairs[way][ROWS * k : ROWS * (k + 1), 0:LANES] = value
                right_pairs[way][ROWS * k : ROWS * (k + 1), LANES : 2 * LANES] = value
        for way in range(WAYS):
            pair_sums[way][...] = lax.dot_general(
                left_pairs[way][...],
                right_pairs[way][...],
                (((1,), (1,)), ((), ())),
                preferred_element_type=F32,
            )
        for way, tile in enumerate(tiles):
            res_sum = jnp.zeros((MODES, LANES), F32)
            lag_sum = jnp.zeros((MODES, LANES), F32)
            for g in range(TILE_GROUPS):
                total = None
                for q in range(0, ROWS, 8):
                    at = slice(ROWS * g + q, ROWS * g + q + 8)
                    block = pair_sums[way][at, 0:LANES] + pair_sums[way][at, LANES : 2 * LANES]
                    keep = iota((8, LANES), 1) + iota((8, LANES), 0) <= ROWS - 1 - q
                    block = jnp.where(keep, block, 0.0)
                    if q:
                        block = pltpu.roll(block, q, 1)
                    total = block if total is None else total + block
                by_lag = jnp.sum(
                    pltpu.roll(total, 0, 1, stride=1, stride_axis=0), axis=0, keepdims=True
                )
                weighted = power_of(tile, g) * by_lag
                res_sum = jnp.where(
                    lane == GROUP * g, jnp.sum(weighted, axis=1, keepdims=True), res_sum
                )
                lag_sum = jnp.where(
                    lane == GROUP * g,
                    jnp.sum(far_back * weighted, axis=1, keepdims=True),
                    lag_sum,
                )
            local_ref[tile, 2 * MODES : 3 * MODES, :] = res_sum
            local_ref[tile, 3 * MODES : 4 * MODES, :] = lag_sum
        return carry

    lax.fori_loop(0, n // WAYS, correlate, 0)
    local_ref[me, 2 * MODES : 3 * MODES, :] = (
        local_ref[me, 2 * MODES : 3 * MODES, :] + pole * cross_res
    )
    local_ref[me, 3 * MODES : 4 * MODES, :] = (
        local_ref[me, 3 * MODES : 4 * MODES, :] + pole * cross_lag
    )
    each(lambda k: receive_in(k).wait_recv())
    each(lambda k: send_out(k).wait_send())
    each(lambda k: send_in(k).wait_send())


def local_part(n, tokens, cotangent, decay_rate, residue, short_filter):
    channels = tokens.shape[2]
    groups = residue.shape[1]
    half = channels // 2
    vmem = pl.BlockSpec(memory_space=pltpu.VMEM)
    wide_rows = TILE_GROUPS * (HALF + 2 * MODES)
    return pl.pallas_call(
        partial(local_kernel, n),
        in_specs=[vmem] * 5,
        out_specs=[vmem] * 7,
        out_shape=[
            jax.ShapeDtypeStruct(shape, F32)
            for shape in (
                (TABLE_ROWS, channels),
                (3, 8, channels),
                (4, 8, channels),
                (n, 2 * MODES, LANES),
                (n, 4 * MODES, LANES),
                (2, ROWS, channels),
                (n, 2 * MODES, LANES),
            )
        ],
        scratch_shapes=[
            pltpu.VMEM((TABLE_ROWS, groups), F32),
            pltpu.VMEM((3, 16, half), BF16),
            pltpu.VMEM((4, 16, half), BF16),
            pltpu.VMEM((3, 16, half), BF16),
            pltpu.VMEM((4, 16, half), BF16),
            pltpu.VMEM((n, 2 * MODES, LANES), F32),
            pltpu.VMEM((n, 2 * MODES, LANES), F32),
            pltpu.VMEM((n, wide_rows, 3 * LANES), BF16),
            pltpu.VMEM((n, 3 * ROWS, 4 * LANES), BF16),
            pltpu.VMEM((3, ROWS + 8, LANES), F32),
            pltpu.VMEM((ROWS, 2 * LANES * 4), BF16),
        ]
        + [pltpu.VMEM((TILE_GROUPS * HALF, 4 * LANES), F32)] * WAYS
        + [pltpu.VMEM((TILE_GROUPS * ROWS, 2 * LANES), BF16)] * WAYS
        + [pltpu.VMEM((2 * ROWS, 2 * LANES), BF16)] * WAYS
        + [pltpu.VMEM((TILE_GROUPS * ROWS, 2 * LANES), F32)] * WAYS
        + [pltpu.SemaphoreType.DMA((2,))] * 2
        + [pltpu.SemaphoreType.DMA((n,))] * 4,
        compiler_params=pltpu.CompilerParams(
            collective_id=0, has_side_effects=True, vmem_limit_bytes=60 * 2**20
        ),
        name="local",
    )(tokens, cotangent, decay_rate, residue, short_filter)


def finish_kernel(
    tiles, proj_ref, cot_ref, before_ref, after_ref, wide_ref, ends_ref, local_ref,
    near_ref, into_ref, gated_ref, grad_ref, sums_ref,
    pads, feats, grads, lefts, rights, fars, flip_parts, mixers, sums,
):
    def spans(tile):
        return slice(tile * LANES, (tile + 1) * LANES)

    for tile in range(tiles):
        lanes = spans(tile)
        pad = pads.at[tile]
        load_tokens(pad, proj_ref, before_ref, lanes)
        for i in range(3):
            pad[i, 8 + ROWS : 16 + ROWS, :] = after_ref[i, :, lanes]
        taps = tap_rows(wide_ref, lanes)
        for start in range(0, ROWS, 32):
            for i in range(3):
                feats[tile, i, start : start + 32, :] = feature(pad, taps, i, start, 32)
        pick = iota((MODES, LANES), 1) % MODES == iota((MODES, LANES), 0)

        def across(row):
            block = wide_ref[row : row + MODES, lanes]
            return jnp.sum(jnp.where(pick, block, 0.0), axis=0, keepdims=True)

        ahead = (iota((ROWS, LANES), 0) + 1).astype(F32)
        high, low = split(across(RESIDUE) * jnp.exp(-across(DECAY) * ahead))
        lefts[tile, :, 0:LANES] = high
        lefts[tile, :, LANES : 2 * LANES] = low
        lefts[tile, :, 2 * LANES : 3 * LANES] = high
        high, low = split(
            jnp.concatenate(
                [into_ref[tile, 0:MODES, :], into_ref[tile, MODES : 2 * MODES, :]], axis=1
            )
        )
        for g in range(TILE_GROUPS):
            keep = in_group(MODES, 2 * LANES, g)
            chosen = jnp.where(keep, high, jnp.zeros_like(high))
            begin = MODES * g
            rights[tile, begin : begin + MODES, :] = chosen
            rights[tile, ROWS + begin : ROWS + begin + MODES, :] = chosen
            rights[tile, 2 * ROWS + begin : 2 * ROWS + begin + MODES, :] = jnp.where(
                keep, low, jnp.zeros_like(low)
            )
    for tile in range(tiles):
        fars[tile] = dot(lefts[tile], rights[tile])
    for tile in range(tiles):
        lanes = spans(tile)
        long_conv = near_ref[0, :, lanes] + fars[tile, :, 0:LANES]
        high, low = split(near_ref[1, :, lanes] + fars[tile, :, LANES : 2 * LANES])
        flip_parts[0:ROWS, lanes] = high
        flip_parts[ROWS : 2 * ROWS, lanes] = low
        gated_ref[:, lanes] = (feats[tile, 0] * long_conv).astype(BF16)
        grads[tile, 0, 0:ROWS, :] = cot_ref[:, lanes].astype(F32) * long_conv
    flip = flip_matrix()
    mixers[...] = dot(jnp.concatenate([flip, flip], axis=1), flip_parts[...])

    for tile in range(tiles):
        lanes = spans(tile)
        pad = pads.at[tile]
        grad = grads.at[tile]
        taps = tap_rows(wide_ref, lanes)
        decay = wide_ref[DECAY : DECAY + MODES, lanes]
        residue = wide_ref[RESIDUE : RESIDUE + MODES, lanes]
        state = into_ref[tile, 0:MODES, :]
        adjoint = into_ref[tile, MODES : 2 * MODES, :]
        grad[1, 0:ROWS, :] = mixers[:, lanes] * feats[tile, 2]
        grad[2, 0:ROWS, :] = mixers[:, lanes] * feats[tile, 1]

        pole = jnp.exp(-decay)
        inverse = jnp.exp(decay)
        next_feat = [feature(pad, taps, i, ROWS, 8) for i in range(3)]
        next_cot = after_ref[3, :, lanes]
        next_in = next_feat[1] * next_feat[2]
        next_grad = next_cot * next_feat[0]
        whole = jnp.exp(-decay * float(ROWS))
        behind = residue * pole * (whole * state + ends_ref[tile, 0:MODES, :])
        beyond = residue * adjoint
        lag_pos = residue
        lag_neg = residue * inverse
        conv_rows, mixer_rows, filters, filters_neg = [], [], [], []
        for k in range(TAPS - 1):
            filters.append(jnp.sum(lag_pos, axis=0, keepdims=True))
            filters_neg.append(jnp.sum(lag_neg, axis=0, keepdims=True))
            conv = jnp.sum(behind, axis=0, keepdims=True)
            mixer = jnp.sum(beyond, axis=0, keepdims=True)
            for j in range(k + 1):
                conv = conv + filters[k - j] * next_in[j : j + 1]
            for j in range(k):
                mixer = mixer - filters_neg[k - j - 1] * next_grad[j : j + 1]
            conv_rows.append(conv)
            mixer_rows.append(mixer)
            lag_pos, lag_neg = lag_pos * pole, lag_neg * inverse
            behind, beyond = behind * pole, beyond * inverse
        blank = jnp.zeros((8 - (TAPS - 1), LANES), F32)
        next_conv = jnp.concatenate(conv_rows + [blank], axis=0)
        next_mixer = jnp.concatenate(mixer_rows + [blank], axis=0)
        grad[0, ROWS : ROWS + 8, :] = next_cot * next_conv
        grad[1, ROWS : ROWS + 8, :] = next_mixer * next_feat[2]
        grad[2, ROWS : ROWS + 8, :] = next_mixer * next_feat[1]

        step = 32
        short = []
        for i in range(3):
            totals = [None] * TAPS
            for start in range(0, ROWS, step):
                rows = slice(start, start + step)
                own = grad[i, rows, :]
                total = None
                for j in range(TAPS):
                    term = taps[TAPS * i + j] * grad[i, start + j : start + j + step, :]
                    total = term if total is None else total + term
                    product = own * pad[i, 8 + start - j : 8 + start - j + step, :]
                    part = product[0:8]
                    for r in range(8, step, 8):
                        part = part + product[r : r + 8]
                    totals[j] = part if totals[j] is None else totals[j] + part
                grad_ref[i, rows, lanes] = total.astype(BF16)
            short += [jnp.sum(part, axis=0, keepdims=True) for part in totals]
        short.append(jnp.zeros((3, LANES), F32))
        lag_sum = local_ref[tile, 3 * MODES : 4 * MODES, :] + pole * (
            local_ref[tile, MODES : 2 * MODES, :] * state + local_ref[tile, 0:MODES, :] * adjoint
        )
        begin = TABLE_ROWS * tile
        sums[begin : begin + 24, :] = jnp.concatenate(short, axis=0)
        sums[begin + 24 : begin + 40, :] = local_ref[tile, 2 * MODES : 3 * MODES, :]
        sums[begin + 40 : begin + 56, :] = lag_sum

    high, low = split(sums[...])
    member = (iota((2 * LANES, LANES), 0) % LANES) // GROUP == iota((2 * LANES, LANES), 1)
    by_group = dot(jnp.concatenate([high, low], axis=1), member.astype(F32).astype(BF16))
    for tile in range(tiles):
        begin = TABLE_ROWS * tile
        packed = by_group[begin : begin + 8]
        for r in range(8, TABLE_ROWS, 8):
            packed = packed + pltpu.roll(by_group[begin + r : begin + r + 8], r, 1)
        sums_ref[tile] = packed


def finish(tokens, cotangent, wide, before, after, ends, local, near, into, block):
    channels = tokens.shape[2]
    tiles = block // LANES
    count = channels // LANES

    def per_tile(rows):
        return pl.BlockSpec((tiles, rows, LANES), lambda t: (t, 0, 0))

    def stack(k, rows):
        return pl.BlockSpec((k, rows, block), lambda t: (0, 0, t))

    plane = pl.BlockSpec((ROWS, block), lambda t: (0, t))
    return pl.pallas_call(
        partial(finish_kernel, tiles),
        grid=(channels // block,),
        in_specs=[
            stack(3, ROWS),
            plane,
            stack(3, 8),
            stack(4, 8),
            pl.BlockSpec((TABLE_ROWS, block), lambda t: (0, t)),
            per_tile(2 * MODES),
            per_tile(4 * MODES),
            stack(2, ROWS),
            per_tile(2 * MODES),
        ],
        out_specs=[plane, stack(3, ROWS), per_tile(8)],
        out_shape=[
            jax.ShapeDtypeStruct((ROWS, channels), BF16),
            jax.ShapeDtypeStruct((3, ROWS, channels), BF16),
            jax.ShapeDtypeStruct((count, 8, LANES), F32),
        ],
        scratch_shapes=[
            pltpu.VMEM((tiles, 3, ROWS + 16, LANES), F32),
            pltpu.VMEM((tiles, 3, ROWS, LANES), F32),
            pltpu.VMEM((tiles, 3, ROWS + 8, LANES), F32),
            pltpu.VMEM((tiles, ROWS, 3 * LANES), BF16),
            pltpu.VMEM((tiles, 3 * ROWS, 2 * LANES), BF16),
            pltpu.VMEM((tiles, ROWS, 2 * LANES), F32),
            pltpu.VMEM((2 * ROWS, tiles * LANES), BF16),
            pltpu.VMEM((ROWS, tiles * LANES), F32),
            pltpu.VMEM((tiles * TABLE_ROWS, LANES), F32),
        ],
        compiler_params=pltpu.CompilerParams(vmem_limit_bytes=48 * 2**20),
        name="finish",
    )(tokens, cotangent, before, after, wide, ends, local, near, into)


def total_kernel(
    n, m, nx, ny, part_ref, out_ref, packed, got, mine_sum, rows, s_a, r_a, s_b, r_b, s_c, r_c
):
    me, genome = lax.axis_index("ctx"), lax.axis_index("seq")
    x, y, z = lax.rem(me, nx), lax.rem(lax.div(me, nx), ny), lax.div(me, nx * ny)
    a, b = ny * m, n // ny
    my_a, my_b = y * m + genome, z * nx + x

    def id_a(k):
        return {"ctx": (z * ny + lax.div(k, m)) * nx + x, "seq": lax.rem(k, m)}

    def id_b(k):
        return {"ctx": (lax.div(k, nx) * ny + y) * nx + lax.rem(k, nx), "seq": genome}

    def ahead(mine, count, k):
        return lax.rem(mine + k, count)

    def behind(mine, count, k):
        return lax.rem(mine + count - k, count)

    def each(count, action):
        def run(k, carry):
            action(k)
            return carry

        lax.fori_loop(1, count, run, 0)

    def remote(source, target, send_sem, recv_sem, to):
        return pltpu.make_async_remote_copy(
            src_ref=source,
            dst_ref=target,
            send_sem=send_sem,
            recv_sem=recv_sem,
            device_id=to,
            device_id_type=MESH,
        )

    barrier = pltpu.get_barrier_semaphore()

    def greet(to):
        pl.semaphore_signal(barrier, inc=1, device_id=to, device_id_type=MESH)

    each(a, lambda k: greet(id_a(ahead(my_a, a, k))))
    each(b, lambda k: greet(id_b(ahead(my_b, b, k))))
    share = n // 2 // a
    for k in range(n // 2):
        packed[k // share, k % share] = part_ref[2 * k] + pltpu.roll(
            part_ref[2 * k + 1], LANES // 2, 1
        )
    got[my_a] = packed[my_a]
    pl.semaphore_wait(barrier, a - 1 + b - 1)

    def first(k, to, slot):
        return remote(packed.at[to], got.at[slot], s_a.at[k], r_a.at[slot], id_a(to))

    def second(k, to, slot):
        return remote(mine_sum, rows.at[slot], s_b.at[k], r_b.at[slot], id_b(to))

    def third(k, to, slot):
        return remote(out_ref.at[my_a], out_ref.at[slot], s_c.at[k], r_c.at[slot], id_a(to))

    def start(mine, count, copy):
        each(count, lambda k: copy(k, ahead(mine, count, k), mine).start())

    def arrive(mine, count, copy):
        each(
            count,
            lambda k: copy(k, behind(mine, count, k), behind(mine, count, k)).wait_recv(),
        )

    def sent(mine, count, copy):
        each(count, lambda k: copy(k, ahead(mine, count, k), mine).wait_send())

    start(my_a, a, first)
    arrive(my_a, a, first)
    total = got[0]
    for d in range(1, a):
        total = total + got[d]
    mine_sum[...] = total
    rows[my_b] = total
    start(my_b, b, second)
    arrive(my_b, b, second)
    total = rows[0]
    for d in range(1, b):
        total = total + rows[d]
    out_ref[my_a] = total
    start(my_a, a, third)
    arrive(my_a, a, third)
    sent(my_a, a, first)
    sent(my_b, b, second)
    sent(my_a, a, third)


def total_sums(n, m, parts):
    ny = 2
    nx = min(4, n // ny)
    a, b = ny * m, n // ny
    share = n // 2 // a
    vmem = pl.BlockSpec(memory_space=pltpu.VMEM)
    dma = pltpu.SemaphoreType.DMA
    return pl.pallas_call(
        partial(total_kernel, n, m, nx, ny),
        out_shape=jax.ShapeDtypeStruct((a, share, 8, LANES), F32),
        in_specs=[vmem],
        out_specs=vmem,
        scratch_shapes=[
            pltpu.VMEM((a, share, 8, LANES), F32),
            pltpu.VMEM((a, share, 8, LANES), F32),
            pltpu.VMEM((share, 8, LANES), F32),
            pltpu.VMEM((b, share, 8, LANES), F32),
            dma((a,)),
            dma((a,)),
            dma((b,)),
            dma((b,)),
            dma((a,)),
            dma((a,)),
        ],
        compiler_params=pltpu.CompilerParams(
            collective_id=1, has_side_effects=True, vmem_limit_bytes=16 * 2**20
        ),
        name="totals",
    )(parts)


def per_device(projected, cotangent, short_filter, residue, decay_rate):
    n, m = lax.axis_size("ctx"), lax.axis_size("seq")
    tokens, upstream = projected[0], cotangent[0]
    groups = residue.shape[1]
    block = min(tokens.shape[2], 512)
    known = local_part(n, tokens, upstream, decay_rate, residue, short_filter)
    gated, grad_tokens, sums = finish(tokens, upstream, *known, block)
    sums = total_sums(n, m, sums)
    sums = sums.reshape(n // 2, 8, 2, 8, TILE_GROUPS).transpose(3, 1, 0, 2, 4)
    sums = sums.reshape(64, groups) / float(ROWS * n * m)
    grad_short = sums[0 : 3 * TAPS].reshape(3, TAPS, groups)
    grad_residue = sums[24 : 24 + MODES]
    grad_log_decay = -residue * decay_rate * sums[40 : 40 + MODES]
    return gated[None], grad_tokens[None], grad_short, grad_residue, grad_log_decay


def solution(mesh):
    placed = (P("seq", None, "ctx", None), P("seq", "ctx", None), P(), P(), P())
    return jax.shard_map(
        per_device,
        mesh=mesh,
        in_specs=placed,
        out_specs=(P("seq", "ctx", None), P("seq", None, "ctx", None), P(), P(), P()),
        check_vma=False,
    )
```

time: 989 us -> 117 us (0.12)
  local copies, waits for them, and re-layouts: 267 us -> 11.6 us
  other arithmetic: 214 us -> 0.62 us
  matrix products: 202 us -> 0 us
  blocking collectives: 152 us -> 0 us
  waiting for transfers between devices: 121 us -> 0 us
  Pallas kernels: 0 us -> 103 us
  between operations: 15 us -> 0.73 us
    dot_general x15 -> x0, matrix products: 202 us -> none  [the longest x1 30.4 us: make_tables(): jnp.einsum('mgi,mgj->gij', residue[:, :, None] * powers, inverse, precisi...]
    all_gather x3 -> x0, waiting for transfers between devices: 121 us -> none  [prefix(): pieces = jax.tree.map(lambda part: lax.all_gather(part, axis), value)]
    select_n x62 -> x0, other arithmetic: 113 us -> none  [step(): jnp.where(position < mine, new, old)]
    pallas_call x0 -> x3, Pallas kernels: none -> 103 us  [the longest x1 67.3 us: local_part(): pl.pallas_call(partial(local_kernel, n), in_specs=[vmem] * 5, out_specs=[...]
    neg x63 -> x0, local copies, waits for them, and re-layouts: 96.6 us -> none  [the longest x62 96.5 us: join_forward(): factor = jnp.exp(-decay_wide * latter[2])]
    unnamed x1 -> x0, blocking collectives: 82.1 us -> none
    psum x1 -> x0, blocking collectives: 69.8 us -> none  [per_device(): lax.psum((short_part, grad_res, grad_lag), ('ctx', 'seq'))]
    broadcast_in_dim x63 -> x0, local copies, waits for them, and re-layouts: 39 us -> none  [the longest x62 37 us: per_device(): decay_wide = jnp.repeat(decay_rate, GROUP, axis=1)]
  transfers between devices with their start and end apart: 5 -> 0, of which waited for: 2 -> 0; matrix products, arithmetic and copies ran while one was open for 19% -> 0% of each run, Pallas kernels for 0% -> 0%
where the time goes in v2:
time: 117 us; the launch traced here: 116 us
  Pallas kernels  103 us (88%)
  local copies, waits for them, and re-layouts  11.6 us (10%)
    pallas_call x1, Pallas kernels, local_part(): pl.pallas_call(partial(local_kernel, n), in_specs=[vmem] * 5, out_specs=[...  67.3 us
    pallas_call x1, Pallas kernels, finish(): pl.pallas_call(partial(finish_kernel, tiles), grid=(channels // block,),...  19.4 us
    pallas_call x1, Pallas kernels, total_sums(): pl.pallas_call(partial(total_kernel, n, m, nx, ny), out_shape=jax.ShapeDt...  16.7 us
    unnamed x18, local copies, waits for them, and re-layouts  6.53 us
    div x3, local copies, waits for them, and re-layouts, per_device(): sums = sums.reshape(64, groups) / float(ROWS * n * m)  2.59 us

profile of v2, /device:TPU:1, one launch (start us, length us, event | category | flops | bytes accessed | tf_op | source)
XLA Modules:
  0.0 116.4 jit_solution(5807659112818265926)
XLA Ops:
  0.6 0.0 copy-start
  0.6 67.3 %local.1 = (f32[56,4096]{1,0:T(8,128)}, f32[3,8,4096]{2,1,0:T(8,128)}, f32[4,8,4096]{2,1,0:T(8,128)}, f32[32,32,128]{2,1,0:T(8,128)}, f32[32,64,128]{2,1,0:T(8,1...) custom-call(bf16[3,128,4096]{2,1,0:T(8,128)(2,1)} %bitcast.9, bf16[128,4096]{1,0:T(8,128)(2,1)} %bitcast.7, ...), custom_call_target="tpu_custom_call" | custom-call | tf_op jit(solution)/shard_map/local/pallas_call | solution.py:398
  68.0 0.0 copy-done
  68.0 0.0 copy-start.1
  68.0 1.2 %copy-done.1 = f32[32,64,128]{2,1,0:T(8,128)S(1)} copy-done((f32[32,64,128]{2,1,0:T(8,128)S(1)}, f32[32,64,128]{2,1,0:T(8,128)}, u32[]{:S(2)}) %copy-start.1) | copy-done | bytes 1048600
  69.2 0.0 copy-start.2
  69.2 1.2 %copy-done.2 = f32[56,4096]{1,0:T(8,128)S(1)} copy-done((f32[56,4096]{1,0:T(8,128)S(1)}, f32[56,4096]{1,0:T(8,128)}, u32[]{:S(2)}) %copy-start.2) | copy-done | bytes 917528
  70.4 0.0 copy-start.3
  70.4 1.0 copy-done.3
  71.4 0.0 copy-start.4
  71.4 1.0 copy-done.4
  72.5 0.0 copy-start.5
  72.5 1.0 copy-done.5
  73.5 0.0 copy-start.6
  73.5 1.0 copy-done.6
  74.5 19.4 %finish.1 = (bf16[128,4096]{1,0:T(8,128)(2,1)}, bf16[3,128,4096]{2,1,0:T(8,128)(2,1)}, f32[32,8,128]{2,1,0:T(8,128)S(1)}) custom-call(bf16[3,128,4096]{2,1,0:T(8,128)(2,1)} %bitcast.10, bf16[128,4096]{1,0:T(8,128)(2,1)S(1)} %bitcast.8, f32[3,8,4096]{2,1,0:T(8,128)S(1)} %copy-done.6, f32[4,8,4096]{2,1,0:T(8,128)S(1)} %copy-done.3, f32[56,4096]{1,0:T(8,128)S(1)} %copy-done.2, ...), custom_call_target="tpu_custom_call" | custom-call | tf_op jit(solution)/shard_map/finish/pallas_call | solution.py:590
  93.9 16.7 %totals.1 = f32[8,2,8,128]{3,2,1,0:T(8,128)S(1)} custom-call(f32[32,8,128]{2,1,0:T(8,128)S(1)} %get-tuple-element.24.part_ref), custom_call_target="tpu_custom_call" | custom-call | tf_op jit(solution)/shard_map/totals/pallas_call | solution.py:726
  110.6 0.0 copy-start.7
  110.6 0.0 copy-start.8
  110.6 0.6 div.14
  111.2 0.3 fusion
  111.5 0.5 copy.12
  112.1 1.5 %div.16 = f32[64,256]{1,0:T(8,128)S(1)} reshape(f32[8,8,16,2,8]{4,3,2,1,0:T(2,128)S(1)} %copy.12) | data formatting | bytes 131072 | tf_op jit(solution)/shard_map/div | solution.py:759
  113.5 0.6 reshape.21
  114.2 0.1 copy.14
  114.3 0.4 slice.19
  114.7 0.0 copy-done.7
  114.7 0.0 copy-done.8
  114.7 0.6 multiply_multiply_fusion
  115.3 0.1 copy.13
  115.4 1.0 slice.17
  (2 shorter events, 0.0 us)
Async XLA Ops:
  0.6 67.3 %copy-start = (bf16[1,128,4096]{2,1,0:T(8,128)(2,1)S(1)}, bf16[1,128,4096]{2,1,0:T(8,128)(2,1)}, u32[]{:S(2)}) copy-start(bf16[1,128,4096]{2,1,0:T(8,128)(2,1)} %param.6) | copy-start | bytes 3145732
  68.0 1.2 %copy-start.1 = (f32[32,64,128]{2,1,0:T(8,128)S(1)}, f32[32,64,128]{2,1,0:T(8,128)}, u32[]{:S(2)}) copy-start(f32[32,64,128]{2,1,0:T(8,128)} %get-tuple-element.19.local_ref) | copy-start | bytes 3145732
  69.2 1.2 %copy-start.2 = (f32[56,4096]{1,0:T(8,128)S(1)}, f32[56,4096]{1,0:T(8,128)}, u32[]{:S(2)}) copy-start(f32[56,4096]{1,0:T(8,128)} %get-tuple-element.17.wide_ref) | copy-start | bytes 2752516
  70.4 1.0 copy-start.3
  71.4 1.0 copy-start.4
  72.5 1.0 copy-start.5
  73.5 1.0 copy-start.6
  110.6 4.1 %copy-start.7 = (f32[16,256]{1,0:T(8,128)S(1)}, f32[16,256]{1,0:T(8,128)}, u32[]{:S(2)}) copy-start(f32[16,256]{1,0:T(8,128)} %decay_ref.1) | copy-start | bytes 49156
  110.6 4.1 %copy-start.8 = (f32[16,256]{1,0:T(8,128)S(1)}, f32[16,256]{1,0:T(8,128)}, u32[]{:S(2)}) copy-start(f32[16,256]{1,0:T(8,128)} %residue_ref.1) | copy-start | bytes 49156

commit v3 on v2

--- a/solution.py
+++ b/solution.py
@@ -17,9 +17,12 @@
 MESH = pl.DeviceIdType.MESH
 
 HALF = ROWS // 2
+QUARTER = ROWS // 4
+GROUPED = 4
 WAYS = 2
 
 DECAY, RESIDUE, SHORT, TABLE_ROWS = 0, 16, 32, 56
+SUM_ROWS = 64
 
 
 def split(value):
@@ -103,12 +106,12 @@
 def local_kernel(
     n, proj_ref, cot_ref, decay_ref, residue_ref, short_ref,
     wide_ref, before_ref, after_ref, ends_ref, local_ref, near_ref, into_ref,
-    small, out_f, out_b, got_f, got_b, got, back, tables, rights, pad, parts, *scratch,
+    small, out_f, out_b, got_f, got_b, got, back, tables, streams, pad, parts, *scratch,
 ):
-    products, left_pairs, right_pairs, pair_sums = (
-        scratch[k * WAYS : (k + 1) * WAYS] for k in range(4)
-    )
-    halo_send, halo_recv, s_out, r_out, s_in, r_in = scratch[4 * WAYS :]
+    left_pairs, right_pairs, pair_sums = (scratch[k * WAYS : (k + 1) * WAYS] for k in range(3))
+    scratch = scratch[3 * WAYS :]
+    rights, products, products_low = (scratch[k * GROUPED : (k + 1) * GROUPED] for k in range(3))
+    halo_send, halo_recv, s_out, r_out, s_in, r_in = scratch[3 * GROUPED :]
     me = lax.axis_index("ctx")
     right_dev, left_dev = lax.rem(me + 1, n), lax.rem(me + n - 1, n)
     far_back = (LANES - 1 - iota((MODES, LANES), 1)).astype(F32)
@@ -188,6 +191,14 @@
         return carry
 
     lax.fori_loop(0, n, build_tables, 0)
+    for way in range(GROUPED):
+        for k in range(3):
+            begin = ROWS * k
+            rights[way][begin : begin + HALF, 2 * LANES : 4 * LANES] = jnp.zeros(
+                (HALF, 2 * LANES), BF16
+            )
+    for way in range(WAYS):
+        right_pairs[way][...] = jnp.zeros((2 * ROWS, 8 * LANES), BF16)
 
     for copy in halo:
         copy.wait()
@@ -210,25 +221,26 @@
             rows = slice(start, start + step)
             f = [feature(pad, taps, i, start, step) for i in range(3)]
             high, low = split(f[1] * f[2])
+            streams[tile, rows, 0:LANES] = high
+            streams[tile, rows, LANES : 2 * LANES] = low
             for k, value in enumerate((high, high, low)):
                 begin = ROWS * k + start
-                rights[tile, begin : begin + step, 0:LANES] = value
+                rights[way][begin : begin + step, 0:LANES] = value
                 if start < HALF:
                     begin = begin + HALF
-                    rights[tile, begin : begin + step, 2 * LANES : 3 * LANES] = value
+                    rights[way][begin : begin + step, 2 * LANES : 3 * LANES] = value
             high, low = split(cot_ref[rows, lanes].astype(F32) * f[0])
             begin = 2 * LANES * way
             parts[rows, begin : begin + LANES] = high
             parts[rows, begin + LANES : begin + 2 * LANES] = low
 
-    def place(tile, flipped):
-        blank = jnp.zeros((HALF, 2 * LANES), BF16)
+    def place(tile, way, flipped):
+        streams[tile, :, 2 * LANES : 4 * LANES] = flipped
         for k, column in enumerate((0, 0, LANES)):
             value = flipped[:, column : column + LANES]
             begin = ROWS * k
-            rights[tile, begin : begin + ROWS, LANES : 2 * LANES] = value
-            rights[tile, begin : begin + HALF, 2 * LANES : 4 * LANES] = blank
-            rights[tile, begin + HALF : begin + ROWS, 3 * LANES : 4 * LANES] = value[0:HALF]
+            rights[way][begin : begin + ROWS, LANES : 2 * LANES] = value
+            rights[way][begin + HALF : begin + ROWS, 3 * LANES : 4 * LANES] = value[0:HALF]
 
     modes, both = slice(0, MODES), slice(0, 2 * LANES)
 
@@ -237,27 +249,35 @@
             ends_ref.at[peer_of(k)], got.at[me], s_out.at[k], r_out.at[me], peer_of(k)
         )
 
-    group = 4 if n % 4 == 0 else 2
-
     def begin_tiles(step, carry):
-        ks = [step * group + way for way in range(group)]
+        ks = [step * GROUPED + way for way in range(GROUPED)]
         for way, k in enumerate(ks):
             features(peer_of(k), way)
-        flipped = dot(flip_matrix(), parts[:, 0 : 2 * LANES * group]).astype(BF16)
+        flipped = dot(flip_matrix(), parts[...]).astype(BF16)
         for way, k in enumerate(ks):
-            place(peer_of(k), flipped[:, 2 * LANES * way : 2 * LANES * (way + 1)])
-        states = [
-            dot(tables[peer_of(k), TILE_GROUPS * HALF :, :], rights[peer_of(k), :, both])
-            for k in ks
-        ]
-        for k, state in zip(ks, states):
+            place(peer_of(k), way, flipped[:, 2 * LANES * way : 2 * LANES * (way + 1)])
+        for way, k in enumerate(ks):
             tile = peer_of(k)
-            ends = select_groups(state, 0, MODES, modes, both)
+            products[way][...] = dot(tables[tile], rights[way][:, 0 : 2 * LANES])
+            products_low[way][...] = dot(
+                tables[tile, 0 : TILE_GROUPS * HALF, :], rights[way][:, 2 * LANES : 4 * LANES]
+            )
+        for way, k in enumerate(ks):
+            tile = peer_of(k)
+            first_end = TILE_GROUPS * HALF
+            ends = select_groups(products[way], first_end, MODES, modes, both)
             ends_ref[tile, 0:MODES, :] = ends[:, 0:LANES]
             ends_ref[tile, MODES : 2 * MODES, :] = ends[:, LANES : 2 * LANES]
-            lags = select_groups(state, TILE_GROUPS * MODES, MODES, modes, both)
+            first_lag = first_end + TILE_GROUPS * MODES
+            lags = select_groups(products[way], first_lag, MODES, modes, both)
             local_ref[tile, 0:MODES, :] = lags[:, 0:LANES]
             local_ref[tile, MODES : 2 * MODES, :] = lags[:, LANES : 2 * LANES]
+            for start in range(0, ROWS, 32):
+                source = products[way] if start >= HALF else products_low[way]
+                begin = start % HALF
+                near = select_groups(source, 0, HALF, slice(begin, begin + 32), both)
+                near_ref[0, start : start + 32, lanes_of(tile)] = near[:, 0:LANES]
+                near_ref[1, start : start + 32, lanes_of(tile)] = near[:, LANES : 2 * LANES]
         for k in ks:
 
             @pl.when(k != 0)
@@ -266,81 +286,27 @@
 
         return carry
 
-    lax.fori_loop(0, n // group, begin_tiles, 0)
-
-    def convolve(step, carry):
-        tiles = [step * WAYS + way for way in range(WAYS)]
-        for way, tile in enumerate(tiles):
-            products[way][...] = dot(tables[tile, 0 : TILE_GROUPS * HALF, :], rights[tile])
-        for way, tile in enumerate(tiles):
-            for start in range(0, ROWS, 32):
-                source = start % HALF
-                columns = slice(0, 2 * LANES) if start >= HALF else slice(2 * LANES, 4 * LANES)
-                near = select_groups(
-                    products[way], 0, HALF, slice(source, source + 32), columns
-                )
-                near_ref[0, start : start + 32, lanes_of(tile)] = near[:, 0:LANES]
-                near_ref[1, start : start + 32, lanes_of(tile)] = near[:, LANES : 2 * LANES]
-        return carry
-
-    lax.fori_loop(0, n // WAYS, convolve, 0)
-
-    def receive_out(k):
-        source = lax.rem(me + n - k, n)
-        return remote(ends_ref.at[source], got.at[source], s_out.at[k], r_out.at[source], source)
-
-    def send_in(k):
-        return remote(back.at[peer_of(k)], into_ref.at[me], s_in.at[k], r_in.at[me], peer_of(k))
-
-    def receive_in(k):
-        source = lax.rem(me + n - k, n)
-        return remote(back.at[source], into_ref.at[source], s_in.at[k], r_in.at[source], source)
-
-    got[me] = ends_ref[me]
-    each(lambda k: receive_out(k).wait_recv())
-    decay = wide_ref[DECAY : DECAY + MODES, lanes_of(me)]
-    pole = jnp.exp(-decay)
-    whole = jnp.exp(-decay * float(ROWS))
-    zero = jnp.zeros((MODES, LANES), F32)
-
-    def scan(step, carry):
-        state, lagged, res, lag, beyond = carry
-        for k in range(2):
-            d = step * 2 + k
-            adjoint = got[d, MODES : 2 * MODES, :]
-            back[d, 0:MODES, :] = state
-            res = res + adjoint * state
-            lag = lag + adjoint * (state + float(ROWS) * lagged)
-            state, lagged = whole * state + got[d, 0:MODES, :], whole * (lagged + state)
-            d = n - 1 - d
-            back[d, MODES : 2 * MODES, :] = beyond
-            beyond = whole * beyond + got[d, MODES : 2 * MODES, :]
-        return state, lagged, res, lag, beyond
-
-    _, _, cross_res, cross_lag, _ = lax.fori_loop(0, n // 2, scan, (zero,) * 5)
-    each(lambda k: send_in(k).start())
-    into_ref[me] = back[me]
+    lax.fori_loop(0, n // GROUPED, begin_tiles, 0)
 
     lane = iota((MODES, LANES), 1)
 
     def correlate(step, carry):
         tiles = [step * WAYS + way for way in range(WAYS)]
         for way, tile in enumerate(tiles):
-            flipped = jnp.concatenate(
-                [
-                    rights[tile, 0:ROWS, LANES : 2 * LANES],
-                    rights[tile, 2 * ROWS : 3 * ROWS, LANES : 2 * LANES],
-                ],
-                axis=1,
-            )
-            for g in range(TILE_GROUPS):
-                left_pairs[way][ROWS * g : ROWS * (g + 1), :] = jnp.where(
-                    in_group(ROWS, 2 * LANES, g), flipped, jnp.zeros_like(flipped)
-                )
-            for k in range(2):
-                value = rights[tile, 2 * ROWS * k : 2 * ROWS * k + ROWS, 0:LANES]
-                right_pairs[way][ROWS * k : ROWS * (k + 1), 0:LANES] = value
-                right_pairs[way][ROWS * k : ROWS * (k + 1), LANES : 2 * LANES] = value
+            for h in range(4):
+                at = slice(QUARTER * h, QUARTER * (h + 1))
+                columns = slice(2 * LANES * h, 2 * LANES * (h + 1))
+                flipped = streams[tile, at, 2 * LANES : 4 * LANES]
+                for g in range(TILE_GROUPS):
+                    left_pairs[way][QUARTER * g : QUARTER * (g + 1), columns] = jnp.where(
+                        in_group(QUARTER, 2 * LANES, g), flipped, jnp.zeros_like(flipped)
+                    )
+                keep = ROWS - QUARTER * h
+                for k in range(2):
+                    value = streams[tile, 0:keep, LANES * k : LANES * (k + 1)]
+                    at = slice(ROWS * (k + 1) - keep, ROWS * (k + 1))
+                    for column in (2 * LANES * h, 2 * LANES * h + LANES):
+                        right_pairs[way][at, column : column + LANES] = value
         for way in range(WAYS):
             pair_sums[way][...] = lax.dot_general(
                 left_pairs[way][...],
@@ -353,8 +319,8 @@
             lag_sum = jnp.zeros((MODES, LANES), F32)
             for g in range(TILE_GROUPS):
                 total = None
-                for q in range(0, ROWS, 8):
-                    at = slice(ROWS * g + q, ROWS * g + q + 8)
+                for q in range(0, QUARTER, 8):
+                    at = slice(QUARTER * g + q, QUARTER * g + q + 8)
                     block = pair_sums[way][at, 0:LANES] + pair_sums[way][at, LANES : 2 * LANES]
                     keep = iota((8, LANES), 1) + iota((8, LANES), 0) <= ROWS - 1 - q
                     block = jnp.where(keep, block, 0.0)
@@ -377,7 +343,45 @@
             local_ref[tile, 3 * MODES : 4 * MODES, :] = lag_sum
         return carry
 
-    lax.fori_loop(0, n // WAYS, correlate, 0)
+    lax.fori_loop(0, n // WAYS // 2, correlate, 0)
+
+    def receive_out(k):
+        source = lax.rem(me + n - k, n)
+        return remote(ends_ref.at[source], got.at[source], s_out.at[k], r_out.at[source], source)
+
+    def send_in(k):
+        return remote(back.at[peer_of(k)], into_ref.at[me], s_in.at[k], r_in.at[me], peer_of(k))
+
+    def receive_in(k):
+        source = lax.rem(me + n - k, n)
+        return remote(back.at[source], into_ref.at[source], s_in.at[k], r_in.at[source], source)
+
+    got[me] = ends_ref[me]
+    each(lambda k: receive_out(k).wait_recv())
+    decay = wide_ref[DECAY : DECAY + MODES, lanes_of(me)]
+    pole = jnp.exp(-decay)
+    whole = jnp.exp(-decay * float(ROWS))
+    zero = jnp.zeros((MODES, LANES), F32)
+
+    def scan(step, carry):
+        state, lagged, res, lag, beyond = carry
+        for k in range(2):
+            d = step * 2 + k
+            adjoint = got[d, MODES : 2 * MODES, :]
+            back[d, 0:MODES, :] = state
+            res = res + adjoint * state
+            lag = lag + adjoint * (state + float(ROWS) * lagged)
+            state, lagged = whole * state + got[d, 0:MODES, :], whole * (lagged + state)
+            d = n - 1 - d
+            back[d, MODES : 2 * MODES, :] = beyond
+            beyond = whole * beyond + got[d, MODES : 2 * MODES, :]
+        return state, lagged, res, lag, beyond
+
+    _, _, cross_res, cross_lag, _ = lax.fori_loop(0, n // 2, scan, (zero,) * 5)
+    each(lambda k: send_in(k).start())
+    into_ref[me] = back[me]
+
+    lax.fori_loop(n // WAYS // 2, n // WAYS, correlate, 0)
     local_ref[me, 2 * MODES : 3 * MODES, :] = (
         local_ref[me, 2 * MODES : 3 * MODES, :] + pole * cross_res
     )
@@ -420,14 +424,16 @@
             pltpu.VMEM((n, 2 * MODES, LANES), F32),
             pltpu.VMEM((n, 2 * MODES, LANES), F32),
             pltpu.VMEM((n, wide_rows, 3 * LANES), BF16),
-            pltpu.VMEM((n, 3 * ROWS, 4 * LANES), BF16),
+            pltpu.VMEM((n, ROWS, 4 * LANES), BF16),
             pltpu.VMEM((3, ROWS + 8, LANES), F32),
-            pltpu.VMEM((ROWS, 2 * LANES * 4), BF16),
+            pltpu.VMEM((ROWS, 2 * LANES * GROUPED), BF16),
         ]
-        + [pltpu.VMEM((TILE_GROUPS * HALF, 4 * LANES), F32)] * WAYS
-        + [pltpu.VMEM((TILE_GROUPS * ROWS, 2 * LANES), BF16)] * WAYS
-        + [pltpu.VMEM((2 * ROWS, 2 * LANES), BF16)] * WAYS
-        + [pltpu.VMEM((TILE_GROUPS * ROWS, 2 * LANES), F32)] * WAYS
+        + [pltpu.VMEM((TILE_GROUPS * QUARTER, 8 * LANES), BF16)] * WAYS
+        + [pltpu.VMEM((2 * ROWS, 8 * LANES), BF16)] * WAYS
+        + [pltpu.VMEM((TILE_GROUPS * QUARTER, 2 * LANES), F32)] * WAYS
+        + [pltpu.VMEM((3 * ROWS, 4 * LANES), BF16)] * GROUPED
+        + [pltpu.VMEM((wide_rows, 2 * LANES), F32)] * GROUPED
+        + [pltpu.VMEM((TILE_GROUPS * HALF, 2 * LANES), F32)] * GROUPED
         + [pltpu.SemaphoreType.DMA((2,))] * 2
         + [pltpu.SemaphoreType.DMA((n,))] * 4,
         compiler_params=pltpu.CompilerParams(
@@ -442,6 +448,12 @@
     near_ref, into_ref, gated_ref, grad_ref, sums_ref,
     pads, feats, grads, lefts, rights, fars, flip_parts, mixers, sums,
 ):
+    step_index = pl.program_id(0)
+
+    @pl.when(step_index == 0)
+    def _():
+        sums_ref[...] = jnp.zeros(sums_ref.shape, F32)
+
     def spans(tile):
         return slice(tile * LANES, (tile + 1) * LANES)
 
@@ -559,26 +571,24 @@
         lag_sum = local_ref[tile, 3 * MODES : 4 * MODES, :] + pole * (
             local_ref[tile, MODES : 2 * MODES, :] * state + local_ref[tile, 0:MODES, :] * adjoint
         )
-        begin = TABLE_ROWS * tile
-        sums[begin : begin + 24, :] = jnp.concatenate(short, axis=0)
-        sums[begin + 24 : begin + 40, :] = local_ref[tile, 2 * MODES : 3 * MODES, :]
-        sums[begin + 40 : begin + 56, :] = lag_sum
-
-    high, low = split(sums[...])
-    member = (iota((2 * LANES, LANES), 0) % LANES) // GROUP == iota((2 * LANES, LANES), 1)
-    by_group = dot(jnp.concatenate([high, low], axis=1), member.astype(F32).astype(BF16))
-    for tile in range(tiles):
-        begin = TABLE_ROWS * tile
-        packed = by_group[begin : begin + 8]
-        for r in range(8, TABLE_ROWS, 8):
-            packed = packed + pltpu.roll(by_group[begin + r : begin + r + 8], r, 1)
-        sums_ref[tile] = packed
+        res_sum = local_ref[tile, 2 * MODES : 3 * MODES, :]
+        rest = jnp.zeros((SUM_ROWS - TABLE_ROWS, LANES), F32)
+        high, low = split(jnp.concatenate(short + [res_sum, lag_sum, rest], axis=0))
+        begin = 2 * LANES * tile
+        sums[:, begin : begin + LANES] = high
+        sums[:, begin + LANES : begin + 2 * LANES] = low
+
+    shape = (tiles * 2 * LANES, sums_ref.shape[1])
+    row = iota(shape, 0)
+    owner = (row // (2 * LANES) + step_index * tiles) * TILE_GROUPS + (row % LANES) // GROUP
+    member = (owner == iota(shape, 1)).astype(F32).astype(BF16)
+    sums_ref[...] = sums_ref[...] + dot(sums[...], member)
 
 
 def finish(tokens, cotangent, wide, before, after, ends, local, near, into, block):
     channels = tokens.shape[2]
     tiles = block // LANES
-    count = channels // LANES
+    groups = channels // GROUP
 
     def per_tile(rows):
         return pl.BlockSpec((tiles, rows, LANES), lambda t: (t, 0, 0))
@@ -601,11 +611,11 @@
             stack(2, ROWS),
             per_tile(2 * MODES),
         ],
-        out_specs=[plane, stack(3, ROWS), per_tile(8)],
+        out_specs=[plane, stack(3, ROWS), pl.BlockSpec((SUM_ROWS, groups), lambda t: (0, 0))],
         out_shape=[
             jax.ShapeDtypeStruct((ROWS, channels), BF16),
             jax.ShapeDtypeStruct((3, ROWS, channels), BF16),
-            jax.ShapeDtypeStruct((count, 8, LANES), F32),
+            jax.ShapeDtypeStruct((SUM_ROWS, groups), F32),
         ],
         scratch_shapes=[
             pltpu.VMEM((tiles, 3, ROWS + 16, LANES), F32),
@@ -616,15 +626,16 @@
             pltpu.VMEM((tiles, ROWS, 2 * LANES), F32),
             pltpu.VMEM((2 * ROWS, tiles * LANES), BF16),
             pltpu.VMEM((ROWS, tiles * LANES), F32),
-            pltpu.VMEM((tiles * TABLE_ROWS, LANES), F32),
+            pltpu.VMEM((SUM_ROWS, tiles * 2 * LANES), BF16),
         ],
-        compiler_params=pltpu.CompilerParams(vmem_limit_bytes=48 * 2**20),
+        compiler_params=pltpu.CompilerParams(vmem_limit_bytes=62 * 2**20),
         name="finish",
     )(tokens, cotangent, before, after, wide, ends, local, near, into)
 
 
 def total_kernel(
-    n, m, nx, ny, part_ref, out_ref, packed, got, mine_sum, rows, s_a, r_a, s_b, r_b, s_c, r_c
+    n, m, nx, ny, part_ref, decay_ref, residue_ref, short_ref, res_ref, log_ref,
+    got, mine_sum, rows, full, s_a, r_a, s_b, r_b, s_c, r_c,
 ):
     me, genome = lax.axis_index("ctx"), lax.axis_index("seq")
     x, y, z = lax.rem(me, nx), lax.rem(lax.div(me, nx), ny), lax.div(me, nx * ny)
@@ -667,22 +678,17 @@
 
     each(a, lambda k: greet(id_a(ahead(my_a, a, k))))
     each(b, lambda k: greet(id_b(ahead(my_b, b, k))))
-    share = n // 2 // a
-    for k in range(n // 2):
-        packed[k // share, k % share] = part_ref[2 * k] + pltpu.roll(
-            part_ref[2 * k + 1], LANES // 2, 1
-        )
-    got[my_a] = packed[my_a]
+    got[my_a] = part_ref[my_a]
     pl.semaphore_wait(barrier, a - 1 + b - 1)
 
     def first(k, to, slot):
-        return remote(packed.at[to], got.at[slot], s_a.at[k], r_a.at[slot], id_a(to))
+        return remote(part_ref.at[to], got.at[slot], s_a.at[k], r_a.at[slot], id_a(to))
 
     def second(k, to, slot):
         return remote(mine_sum, rows.at[slot], s_b.at[k], r_b.at[slot], id_b(to))
 
     def third(k, to, slot):
-        return remote(out_ref.at[my_a], out_ref.at[slot], s_c.at[k], r_c.at[slot], id_a(to))
+        return remote(full.at[my_a], full.at[slot], s_c.at[k], r_c.at[slot], id_a(to))
 
     def start(mine, count, copy):
         each(count, lambda k: copy(k, ahead(mine, count, k), mine).start())
@@ -708,31 +714,42 @@
     total = rows[0]
     for d in range(1, b):
         total = total + rows[d]
-    out_ref[my_a] = total
+    full[my_a] = total
     start(my_a, a, third)
     arrive(my_a, a, third)
+    share = full.shape[1]
+    sums = jnp.concatenate([full[k // share, k % share] for k in range(TABLE_ROWS // 8)], axis=0)
+    sums = sums * (1.0 / float(ROWS * n * m))
+    for i in range(3):
+        short_ref[i] = sums[TAPS * i : TAPS * (i + 1)]
+    res_ref[...] = sums[24 : 24 + MODES]
+    log_ref[...] = -residue_ref[...] * decay_ref[...] * sums[40 : 40 + MODES]
     sent(my_a, a, first)
     sent(my_b, b, second)
     sent(my_a, a, third)
 
 
-def total_sums(n, m, parts):
+def total_sums(n, m, parts, decay_rate, residue):
     ny = 2
     nx = min(4, n // ny)
     a, b = ny * m, n // ny
-    share = n // 2 // a
+    share, groups = SUM_ROWS // 8 // a, parts.shape[1]
     vmem = pl.BlockSpec(memory_space=pltpu.VMEM)
     dma = pltpu.SemaphoreType.DMA
     return pl.pallas_call(
         partial(total_kernel, n, m, nx, ny),
-        out_shape=jax.ShapeDtypeStruct((a, share, 8, LANES), F32),
-        in_specs=[vmem],
-        out_specs=vmem,
+        out_shape=[
+            jax.ShapeDtypeStruct((3, TAPS, groups), F32),
+            jax.ShapeDtypeStruct((MODES, groups), F32),
+            jax.ShapeDtypeStruct((MODES, groups), F32),
+        ],
+        in_specs=[vmem] * 3,
+        out_specs=[vmem] * 3,
         scratch_shapes=[
-            pltpu.VMEM((a, share, 8, LANES), F32),
-            pltpu.VMEM((a, share, 8, LANES), F32),
-            pltpu.VMEM((share, 8, LANES), F32),
-            pltpu.VMEM((b, share, 8, LANES), F32),
+            pltpu.VMEM((a, share, 8, groups), F32),
+            pltpu.VMEM((share, 8, groups), F32),
+            pltpu.VMEM((b, share, 8, groups), F32),
+            pltpu.VMEM((a, share, 8, groups), F32),
             dma((a,)),
             dma((a,)),
             dma((b,)),
@@ -744,23 +761,16 @@
             collective_id=1, has_side_effects=True, vmem_limit_bytes=16 * 2**20
         ),
         name="totals",
-    )(parts)
+    )(parts.reshape(a, share, 8, groups), decay_rate, residue)
 
 
 def per_device(projected, cotangent, short_filter, residue, decay_rate):
     n, m = lax.axis_size("ctx"), lax.axis_size("seq")
     tokens, upstream = projected[0], cotangent[0]
-    groups = residue.shape[1]
     block = min(tokens.shape[2], 512)
     known = local_part(n, tokens, upstream, decay_rate, residue, short_filter)
     gated, grad_tokens, sums = finish(tokens, upstream, *known, block)
-    sums = total_sums(n, m, sums)
-    sums = sums.reshape(n // 2, 8, 2, 8, TILE_GROUPS).transpose(3, 1, 0, 2, 4)
-    sums = sums.reshape(64, groups) / float(ROWS * n * m)
-    grad_short = sums[0 : 3 * TAPS].reshape(3, TAPS, groups)
-    grad_residue = sums[24 : 24 + MODES]
-    grad_log_decay = -residue * decay_rate * sums[40 : 40 + MODES]
-    return gated[None], grad_tokens[None], grad_short, grad_residue, grad_log_decay
+    return gated[None], grad_tokens[None], *total_sums(n, m, sums, decay_rate, residue)
 
 
 def solution(mesh):

time: 117 us -> 102 us (0.87)
  local copies, waits for them, and re-layouts: 11.6 us -> 2.67 us
  Pallas kernels: 103 us -> 98.6 us
    pallas_call x1, Pallas kernels: 67.3 us -> 59.2 us  [local_part(): pl.pallas_call(partial(local_kernel, n), in_specs=[vmem] * 5, out_specs=[...]
    unnamed x18 -> x9, local copies, waits for them, and re-layouts: 6.53 us -> 2.67 us
    pallas_call x1, Pallas kernels: 19.4 us -> 22.6 us  [finish(): pl.pallas_call(partial(finish_kernel, tiles), grid=(channels // block,),...]
    div x3 -> x0, local copies, waits for them, and re-layouts: 2.59 us -> none  [per_device(): sums = sums.reshape(64, groups) / float(ROWS * n * m)]
    slice x6 -> x0, local copies, waits for them, and re-layouts: 1.9 us -> none  [the longest x2 1.1 us: per_device(): grad_residue = sums[24:24 + MODES]]
where the time goes in v3:
time: 102 us
  Pallas kernels  98.6 us (97%)
  local copies, waits for them, and re-layouts  2.67 us (3%)
    pallas_call x1, Pallas kernels, local_part(): pl.pallas_call(partial(local_kernel, n), in_specs=[vmem] * 5, out_specs=[...  59.2 us
    pallas_call x1, Pallas kernels, finish(): pl.pallas_call(partial(finish_kernel, tiles), grid=(channels // block,),...  22.6 us
    pallas_call x1, Pallas kernels, total_sums(): pl.pallas_call(partial(total_kernel, n, m, nx, ny), out_shape=[jax.ShapeD...  16.8 us
    unnamed x9, local copies, waits for them, and re-layouts  2.67 us

profile of v3, /device:TPU:1, one launch (start us, length us, event | category | flops | bytes accessed | tf_op | source)
XLA Modules:
  0.0 101.9 jit_solution(14658935166674630372)
XLA Ops:
  0.6 59.2 %local.1 = (f32[56,4096]{1,0:T(8,128)}, f32[3,8,4096]{2,1,0:T(8,128)}, f32[4,8,4096]{2,1,0:T(8,128)}, f32[32,32,128]{2,1,0:T(8,128)}, f32[32,64,128]{2,1,0:T(8,1...) custom-call(bf16[3,128,4096]{2,1,0:T(8,128)(2,1)} %bitcast.6, bf16[128,4096]{1,0:T(8,128)(2,1)} %bitcast.8, ...), custom_call_target="tpu_custom_call" | custom-call | tf_op jit(solution)/shard_map/local/pallas_call | solution.py:402
  59.9 0.0 copy-start
  59.9 0.0 copy-start.1
  59.9 22.6 %finish.1 = (bf16[128,4096]{1,0:T(8,128)(2,1)}, bf16[3,128,4096]{2,1,0:T(8,128)(2,1)}, f32[64,256]{1,0:T(8,128)}) custom-call(bf16[3,128,4096]{2,1,0:T(8,128)(2,1)} %bitcast.7, bf16[128,4096]{1,0:T(8,128)(2,1)} %bitcast.9, f32[3,8,4096]{2,1,0:T(8,128)} %get-tuple-element.18.before_ref, f32[4,8,4096]{2,1,0:T(8,128)} %get-tuple-element.19.after_ref, ...), custom_call_target="tpu_custom_call" | custom-call | tf_op jit(solution)/shard_map/finish/pallas_call | solution.py:600
  82.5 0.0 copy-done
  82.5 0.0 copy-done.1
  82.5 0.0 copy-start.2
  82.5 0.8 copy-done.2
  83.3 16.8 %totals.1 = (f32[3,7,256]{2,1,0:T(8,128)S(1)}, f32[16,256]{1,0:T(8,128)S(1)}, f32[16,256]{1,0:T(8,128)S(1)}) custom-call(f32[8,1,8,256]{3,2,1,0:T(8,128)S(1)} %bitcast.5, f32[16,256]{1,0:T(8,128)S(1)} %copy-done, f32[16,256]{1,0:T(8,128)S(1)} %copy-done.1), custom_call_target="tpu_custom_call" | custom-call | tf_op jit(solution)/shard_map/totals/pallas_call | solution.py:739
  100.1 0.6 copy.13
  100.7 0.6 copy.14
  101.3 0.6 copy.15
Async XLA Ops:
  59.9 22.6 %copy-start = (f32[16,256]{1,0:T(8,128)S(1)}, f32[16,256]{1,0:T(8,128)}, u32[]{:S(2)}) copy-start(f32[16,256]{1,0:T(8,128)} %decay_ref.3) | copy-start | bytes 49156
  59.9 22.6 %copy-start.1 = (f32[16,256]{1,0:T(8,128)S(1)}, f32[16,256]{1,0:T(8,128)}, u32[]{:S(2)}) copy-start(f32[16,256]{1,0:T(8,128)} %residue_ref.3) | copy-start | bytes 49156
  82.5 0.8 copy-start.2

commit v4 on v3

--- a/solution.py
+++ b/solution.py
@@ -104,14 +104,14 @@
 
 
 def local_kernel(
-    n, proj_ref, cot_ref, decay_ref, residue_ref, short_ref,
-    wide_ref, before_ref, after_ref, ends_ref, local_ref, near_ref, into_ref,
-    small, out_f, out_b, got_f, got_b, got, back, tables, streams, pad, parts, *scratch,
+    n, proj_hbm, cot_hbm, decay_ref, residue_ref, short_ref,
+    wide_ref, before_ref, after_ref, ends_ref, local_ref, near_hbm, into_ref, feat_hbm,
+    proj_ref, cot_ref, near_ref, feat_ref, small, out_f, out_b, got_f, got_b, got, back, tables, streams, pad, parts, *scratch,
 ):
     left_pairs, right_pairs, pair_sums = (scratch[k * WAYS : (k + 1) * WAYS] for k in range(3))
     scratch = scratch[3 * WAYS :]
     rights, products, products_low = (scratch[k * GROUPED : (k + 1) * GROUPED] for k in range(3))
-    halo_send, halo_recv, s_out, r_out, s_in, r_in = scratch[3 * GROUPED :]
+    local_sem, halo_send, halo_recv, s_out, r_out, s_in, r_in = scratch[3 * GROUPED :]
     me = lax.axis_index("ctx")
     right_dev, left_dev = lax.rem(me + 1, n), lax.rem(me + n - 1, n)
     far_back = (LANES - 1 - iota((MODES, LANES), 1)).astype(F32)
@@ -136,12 +136,25 @@
             device_id_type=MESH,
         )
 
+    loads = [
+        pltpu.make_async_copy(proj_hbm, proj_ref, local_sem.at[0]),
+        pltpu.make_async_copy(cot_hbm, cot_ref, local_sem.at[1]),
+    ]
+    stores = [
+        pltpu.make_async_copy(near_ref, near_hbm, local_sem.at[2]),
+        pltpu.make_async_copy(feat_ref, feat_hbm, local_sem.at[3]),
+    ]
+    for copy in loads:
+        copy.start()
     barrier = pltpu.get_barrier_semaphore()
     each(
         lambda k: pl.semaphore_signal(
             barrier, inc=1, device_id={"ctx": peer_of(k)}, device_id_type=MESH
         )
     )
+    expand_table(wide_ref, small, decay_ref, residue_ref, short_ref)
+    for copy in loads:
+        copy.wait()
     width = out_f.shape[2]
     for i in range(3):
         tail = proj_ref[i, ROWS - 16 : ROWS, :].astype(F32)[8:16]
@@ -149,7 +162,6 @@
     for i in range(4):
         head = (cot_ref[0:16, :] if i == 3 else proj_ref[i, 0:16, :]).astype(F32)[0:8]
         out_b[i] = jnp.concatenate([head[:, :width], head[:, width:]], axis=0).astype(BF16)
-    expand_table(wide_ref, small, decay_ref, residue_ref, short_ref)
     pl.semaphore_wait(barrier, n - 1)
     halo = [
         remote(out_f, got_f, halo_send.at[0], halo_recv.at[0], right_dev),
@@ -220,6 +232,8 @@
         for start in range(0, ROWS, step):
             rows = slice(start, start + step)
             f = [feature(pad, taps, i, start, step) for i in range(3)]
+            for i in range(3):
+                feat_ref[i, rows, lanes] = f[i]
             high, low = split(f[1] * f[2])
             streams[tile, rows, 0:LANES] = high
             streams[tile, rows, LANES : 2 * LANES] = low
@@ -287,6 +301,8 @@
         return carry
 
     lax.fori_loop(0, n // GROUPED, begin_tiles, 0)
+    for copy in stores:
+        copy.start()
 
     lane = iota((MODES, LANES), 1)
 
@@ -391,6 +407,8 @@
     each(lambda k: receive_in(k).wait_recv())
     each(lambda k: send_out(k).wait_send())
     each(lambda k: send_in(k).wait_send())
+    for copy in stores:
+        copy.wait()
 
 
 def local_part(n, tokens, cotangent, decay_rate, residue, short_filter):
@@ -401,8 +419,9 @@
     wide_rows = TILE_GROUPS * (HALF + 2 * MODES)
     return pl.pallas_call(
         partial(local_kernel, n),
-        in_specs=[vmem] * 5,
-        out_specs=[vmem] * 7,
+        in_specs=[pl.BlockSpec(memory_space=pl.ANY)] * 2 + [vmem] * 3,
+        out_specs=[vmem] * 5 + [pl.BlockSpec(memory_space=pl.ANY), vmem]
+        + [pl.BlockSpec(memory_space=pl.ANY)],
         out_shape=[
             jax.ShapeDtypeStruct(shape, F32)
             for shape in (
@@ -413,9 +432,14 @@
                 (n, 4 * MODES, LANES),
                 (2, ROWS, channels),
                 (n, 2 * MODES, LANES),
+                (3, ROWS, channels),
             )
         ],
         scratch_shapes=[
+            pltpu.VMEM((3, ROWS, channels), BF16),
+            pltpu.VMEM((ROWS, channels), BF16),
+            pltpu.VMEM((2, ROWS, channels), F32),
+            pltpu.VMEM((3, ROWS, channels), F32),
             pltpu.VMEM((TABLE_ROWS, groups), F32),
             pltpu.VMEM((3, 16, half), BF16),
             pltpu.VMEM((4, 16, half), BF16),
@@ -434,6 +458,7 @@
         + [pltpu.VMEM((3 * ROWS, 4 * LANES), BF16)] * GROUPED
         + [pltpu.VMEM((wide_rows, 2 * LANES), F32)] * GROUPED
         + [pltpu.VMEM((TILE_GROUPS * HALF, 2 * LANES), F32)] * GROUPED
+        + [pltpu.SemaphoreType.DMA((4,))]
         + [pltpu.SemaphoreType.DMA((2,))] * 2
         + [pltpu.SemaphoreType.DMA((n,))] * 4,
         compiler_params=pltpu.CompilerParams(
@@ -445,14 +470,10 @@
 
 def finish_kernel(
     tiles, proj_ref, cot_ref, before_ref, after_ref, wide_ref, ends_ref, local_ref,
-    near_ref, into_ref, gated_ref, grad_ref, sums_ref,
-    pads, feats, grads, lefts, rights, fars, flip_parts, mixers, sums,
+    near_ref, into_ref, feat_ref, gated_ref, grad_ref, sums_ref,
+    pads, grads, lefts, rights, fars, sums, placed,
 ):
     step_index = pl.program_id(0)
-
-    @pl.when(step_index == 0)
-    def _():
-        sums_ref[...] = jnp.zeros(sums_ref.shape, F32)
 
     def spans(tile):
         return slice(tile * LANES, (tile + 1) * LANES)
@@ -463,10 +484,6 @@
         load_tokens(pad, proj_ref, before_ref, lanes)
         for i in range(3):
             pad[i, 8 + ROWS : 16 + ROWS, :] = after_ref[i, :, lanes]
-        taps = tap_rows(wide_ref, lanes)
-        for start in range(0, ROWS, 32):
-            for i in range(3):
-                feats[tile, i, start : start + 32, :] = feature(pad, taps, i, start, 32)
         pick = iota((MODES, LANES), 1) % MODES == iota((MODES, LANES), 0)
 
         def across(row):
@@ -497,14 +514,15 @@
     for tile in range(tiles):
         lanes = spans(tile)
         long_conv = near_ref[0, :, lanes] + fars[tile, :, 0:LANES]
-        high, low = split(near_ref[1, :, lanes] + fars[tile, :, LANES : 2 * LANES])
-        flip_parts[0:ROWS, lanes] = high
-        flip_parts[ROWS : 2 * ROWS, lanes] = low
-        gated_ref[:, lanes] = (feats[tile, 0] * long_conv).astype(BF16)
+        for start in range(0, ROWS, 8):
+            rows = slice(start, start + 8)
+            value = near_ref[1, rows, lanes] + fars[tile, rows, LANES : 2 * LANES]
+            turned = jnp.take_along_axis(value, 7 - iota((8, LANES), 0), axis=0)
+            at = slice(ROWS - 8 - start, ROWS - start)
+            grads[tile, 1, at, :] = turned * feat_ref[2, at, lanes]
+            grads[tile, 2, at, :] = turned * feat_ref[1, at, lanes]
+        gated_ref[:, lanes] = (feat_ref[0, :, lanes] * long_conv).astype(BF16)
         grads[tile, 0, 0:ROWS, :] = cot_ref[:, lanes].astype(F32) * long_conv
-    flip = flip_matrix()
-    mixers[...] = dot(jnp.concatenate([flip, flip], axis=1), flip_parts[...])
-
     for tile in range(tiles):
         lanes = spans(tile)
         pad = pads.at[tile]
@@ -514,8 +532,6 @@
         residue = wide_ref[RESIDUE : RESIDUE + MODES, lanes]
         state = into_ref[tile, 0:MODES, :]
         adjoint = into_ref[tile, MODES : 2 * MODES, :]
-        grad[1, 0:ROWS, :] = mixers[:, lanes] * feats[tile, 2]
-        grad[2, 0:ROWS, :] = mixers[:, lanes] * feats[tile, 1]
 
         pole = jnp.exp(-decay)
         inverse = jnp.exp(decay)
@@ -555,12 +571,13 @@
             totals = [None] * TAPS
             for start in range(0, ROWS, step):
                 rows = slice(start, start + step)
-                own = grad[i, rows, :]
+                own = pad[i, 8 + start : 8 + start + step, :]
                 total = None
                 for j in range(TAPS):
-                    term = taps[TAPS * i + j] * grad[i, start + j : start + j + step, :]
+                    ahead_grad = grad[i, start + j : start + j + step, :]
+                    term = taps[TAPS * i + j] * ahead_grad
                     total = term if total is None else total + term
-                    product = own * pad[i, 8 + start - j : 8 + start - j + step, :]
+                    product = own * ahead_grad
                     part = product[0:8]
                     for r in range(8, step, 8):
                         part = part + product[r : r + 8]
@@ -574,18 +591,31 @@
         res_sum = local_ref[tile, 2 * MODES : 3 * MODES, :]
         rest = jnp.zeros((SUM_ROWS - TABLE_ROWS, LANES), F32)
         high, low = split(jnp.concatenate(short + [res_sum, lag_sum, rest], axis=0))
-        begin = 2 * LANES * tile
-        sums[:, begin : begin + LANES] = high
-        sums[:, begin + LANES : begin + 2 * LANES] = low
-
-    shape = (tiles * 2 * LANES, sums_ref.shape[1])
-    row = iota(shape, 0)
-    owner = (row // (2 * LANES) + step_index * tiles) * TILE_GROUPS + (row % LANES) // GROUP
-    member = (owner == iota(shape, 1)).astype(F32).astype(BF16)
-    sums_ref[...] = sums_ref[...] + dot(sums[...], member)
-
-
-def finish(tokens, cotangent, wide, before, after, ends, local, near, into, block):
+        at = slice(SUM_ROWS * tile, SUM_ROWS * (tile + 1))
+        sums[at, 0:LANES] = high
+        sums[at, LANES : 2 * LANES] = low
+
+    member = (iota((2 * LANES, LANES), 0) % LANES) // GROUP == iota((2 * LANES, LANES), 1)
+    by_group = dot(sums[...], member.astype(F32).astype(BF16))
+    total = by_group[0:SUM_ROWS]
+    for tile in range(1, tiles):
+        part = by_group[SUM_ROWS * tile : SUM_ROWS * (tile + 1)]
+        total = total + pltpu.roll(part, TILE_GROUPS * tile, 1)
+    placed[step_index] = total
+
+    @pl.when(step_index == pl.num_programs(0) - 1)
+    def _():
+        groups = sums_ref.shape[1]
+        width = min(groups, LANES)
+        stride = tiles * TILE_GROUPS
+        for begin in range(0, groups, width):
+            total = placed[begin // stride]
+            for k in range(1, width // stride):
+                total = total + pltpu.roll(placed[begin // stride + k], stride * k, 1)
+            sums_ref[:, begin : begin + width] = total[:, 0:width]
+
+
+def finish(tokens, cotangent, wide, before, after, ends, local, near, into, feats, block):
     channels = tokens.shape[2]
     tiles = block // LANES
     groups = channels // GROUP
@@ -610,6 +640,7 @@
             per_tile(4 * MODES),
             stack(2, ROWS),
             per_tile(2 * MODES),
+            stack(3, ROWS),
         ],
         out_specs=[plane, stack(3, ROWS), pl.BlockSpec((SUM_ROWS, groups), lambda t: (0, 0))],
         out_shape=[
@@ -619,18 +650,16 @@
         ],
         scratch_shapes=[
             pltpu.VMEM((tiles, 3, ROWS + 16, LANES), F32),
-            pltpu.VMEM((tiles, 3, ROWS, LANES), F32),
             pltpu.VMEM((tiles, 3, ROWS + 8, LANES), F32),
             pltpu.VMEM((tiles, ROWS, 3 * LANES), BF16),
             pltpu.VMEM((tiles, 3 * ROWS, 2 * LANES), BF16),
             pltpu.VMEM((tiles, ROWS, 2 * LANES), F32),
-            pltpu.VMEM((2 * ROWS, tiles * LANES), BF16),
-            pltpu.VMEM((ROWS, tiles * LANES), F32),
-            pltpu.VMEM((SUM_ROWS, tiles * 2 * LANES), BF16),
+            pltpu.VMEM((tiles * SUM_ROWS, 2 * LANES), BF16),
+            pltpu.VMEM((channels // block, SUM_ROWS, LANES), F32),
         ],
         compiler_params=pltpu.CompilerParams(vmem_limit_bytes=62 * 2**20),
         name="finish",
-    )(tokens, cotangent, before, after, wide, ends, local, near, into)
+    )(tokens, cotangent, before, after, wide, ends, local, near, into, feats)
 
 
 def total_kernel(

time: 102 us -> 94.5 us (0.926)
  Pallas kernels: 98.6 us -> 90.7 us
    pallas_call x1, Pallas kernels: 22.6 us -> 16.9 us  [finish(): pl.pallas_call(partial(finish_kernel, tiles), grid=(channels // block,),...]
    pallas_call x1, Pallas kernels: 59.2 us -> 57 us  [local_part(): pl.pallas_call(partial(local_kernel, n), in_specs=[pl.BlockSpec(memory_sp...]
where the time goes in v4:
time: 94.5 us; the launch traced here: 94.1 us
  Pallas kernels  90.7 us (96%)
  local copies, waits for them, and re-layouts  2.67 us (3%)
    pallas_call x1, Pallas kernels, local_part(): pl.pallas_call(partial(local_kernel, n), in_specs=[pl.BlockSpec(memory_sp...  57 us
    pallas_call x1, Pallas kernels, finish(): pl.pallas_call(partial(finish_kernel, tiles), grid=(channels // block,),...  16.9 us
    pallas_call x1, Pallas kernels, total_sums(): pl.pallas_call(partial(total_kernel, n, m, nx, ny), out_shape=[jax.ShapeD...  16.8 us
    unnamed x9, local copies, waits for them, and re-layouts  2.67 us

profile of v4, /device:TPU:1, one launch (start us, length us, event | category | flops | bytes accessed | tf_op | source)
XLA Modules:
  0.0 94.1 jit_solution(7405309856845357484)
XLA Ops:
  0.6 57.0 %local.1 = (f32[56,4096]{1,0:T(8,128)}, f32[3,8,4096]{2,1,0:T(8,128)}, f32[4,8,4096]{2,1,0:T(8,128)}, f32[32,32,128]{2,1,0:T(8,128)}, f32[32,64,128]{2,1,0:T(8,1...) custom-call(bf16[3,128,4096]{2,1,0:T(8,128)(2,1)} %bitcast.6, ...), custom_call_target="tpu_custom_call" | custom-call | tf_op jit(solution)/shard_map/local/pallas_call | solution.py:420
  57.6 0.0 copy-start
  57.6 0.0 copy-start.1
  57.7 16.9 %finish.1 = (bf16[128,4096]{1,0:T(8,128)(2,1)}, bf16[3,128,4096]{2,1,0:T(8,128)(2,1)}, f32[64,256]{1,0:T(8,128)}) custom-call(bf16[3,128,4096]{2,1,0:T(8,128)(2,1)} %bitcast.7, bf16[128,4096]{1,0:T(8,128)(2,1)} %bitcast.9, f32[3,8,4096]{2,1,0:T(8,128)} %get-tuple-element.19.before_ref, f32[4,8,4096]{2,1,0:T(8,128)} %get-tuple-element.20.after_ref, ...), custom_call_target="tpu_custom_call" | custom-call | tf_op jit(solution)/shard_map/finish/pallas_call | solution.py:630
  74.6 0.0 copy-done
  74.6 0.0 copy-done.1
  74.6 0.0 copy-start.2
  74.6 0.8 copy-done.2
  75.4 16.8 %totals.1 = (f32[3,7,256]{2,1,0:T(8,128)S(1)}, f32[16,256]{1,0:T(8,128)S(1)}, f32[16,256]{1,0:T(8,128)S(1)}) custom-call(f32[8,1,8,256]{3,2,1,0:T(8,128)S(1)} %bitcast.5, f32[16,256]{1,0:T(8,128)S(1)} %copy-done, f32[16,256]{1,0:T(8,128)S(1)} %copy-done.1), custom_call_target="tpu_custom_call" | custom-call | tf_op jit(solution)/shard_map/totals/pallas_call | solution.py:768
  92.3 0.6 copy.13
  92.9 0.6 copy.14
  93.5 0.6 copy.15
Async XLA Ops:
  57.6 16.9 %copy-start = (f32[16,256]{1,0:T(8,128)S(1)}, f32[16,256]{1,0:T(8,128)}, u32[]{:S(2)}) copy-start(f32[16,256]{1,0:T(8,128)} %decay_ref.3) | copy-start | bytes 49156
  57.6 16.9 %copy-start.1 = (f32[16,256]{1,0:T(8,128)S(1)}, f32[16,256]{1,0:T(8,128)}, u32[]{:S(2)}) copy-start(f32[16,256]{1,0:T(8,128)} %residue_ref.3) | copy-start | bytes 49156
  74.6 0.8 copy-start.2

commit v5 on v4

--- a/solution.py
+++ b/solution.py
@@ -260,7 +260,7 @@
 
     def send_out(k):
         return remote(
-            ends_ref.at[peer_of(k)], got.at[me], s_out.at[k], r_out.at[me], peer_of(k)
+            ends_ref.at[peer_of(k)], got.at[me], s_out.at[0], r_out.at[0], peer_of(k)
         )
 
     def begin_tiles(step, carry):
@@ -361,19 +361,14 @@
 
     lax.fori_loop(0, n // WAYS // 2, correlate, 0)
 
-    def receive_out(k):
-        source = lax.rem(me + n - k, n)
-        return remote(ends_ref.at[source], got.at[source], s_out.at[k], r_out.at[source], source)
-
     def send_in(k):
-        return remote(back.at[peer_of(k)], into_ref.at[me], s_in.at[k], r_in.at[me], peer_of(k))
-
-    def receive_in(k):
-        source = lax.rem(me + n - k, n)
-        return remote(back.at[source], into_ref.at[source], s_in.at[k], r_in.at[source], source)
-
+        return remote(back.at[peer_of(k)], into_ref.at[me], s_in.at[0], r_in.at[0], peer_of(k))
+
+    others = pl.ds(0, n - 1)
+    all_out = remote(ends_ref.at[others], got.at[others], s_out.at[0], r_out.at[0], right_dev)
+    all_in = remote(back.at[others], into_ref.at[others], s_in.at[0], r_in.at[0], right_dev)
     got[me] = ends_ref[me]
-    each(lambda k: receive_out(k).wait_recv())
+    all_out.wait_recv()
     decay = wide_ref[DECAY : DECAY + MODES, lanes_of(me)]
     pole = jnp.exp(-decay)
     whole = jnp.exp(-decay * float(ROWS))
@@ -381,8 +376,8 @@
 
     def scan(step, carry):
         state, lagged, res, lag, beyond = carry
-        for k in range(2):
-            d = step * 2 + k
+        for k in range(4):
+            d = step * 4 + k
             adjoint = got[d, MODES : 2 * MODES, :]
             back[d, 0:MODES, :] = state
             res = res + adjoint * state
@@ -393,7 +388,7 @@
             beyond = whole * beyond + got[d, MODES : 2 * MODES, :]
         return state, lagged, res, lag, beyond
 
-    _, _, cross_res, cross_lag, _ = lax.fori_loop(0, n // 2, scan, (zero,) * 5)
+    _, _, cross_res, cross_lag, _ = lax.fori_loop(0, n // 4, scan, (zero,) * 5)
     each(lambda k: send_in(k).start())
     into_ref[me] = back[me]
 
@@ -404,9 +399,9 @@
     local_ref[me, 3 * MODES : 4 * MODES, :] = (
         local_ref[me, 3 * MODES : 4 * MODES, :] + pole * cross_lag
     )
-    each(lambda k: receive_in(k).wait_recv())
-    each(lambda k: send_out(k).wait_send())
-    each(lambda k: send_in(k).wait_send())
+    all_in.wait_recv()
+    all_out.wait_send()
+    all_in.wait_send()
     for copy in stores:
         copy.wait()
 
@@ -460,7 +455,7 @@
         + [pltpu.VMEM((TILE_GROUPS * HALF, 2 * LANES), F32)] * GROUPED
         + [pltpu.SemaphoreType.DMA((4,))]
         + [pltpu.SemaphoreType.DMA((2,))] * 2
-        + [pltpu.SemaphoreType.DMA((n,))] * 4,
+        + [pltpu.SemaphoreType.DMA((1,))] * 4,
         compiler_params=pltpu.CompilerParams(
             collective_id=0, has_side_effects=True, vmem_limit_bytes=60 * 2**20
         ),
@@ -680,9 +675,6 @@
     def ahead(mine, count, k):
         return lax.rem(mine + k, count)
 
-    def behind(mine, count, k):
-        return lax.rem(mine + count - k, count)
-
     def each(count, action):
         def run(k, carry):
             action(k)
@@ -710,42 +702,40 @@
     got[my_a] = part_ref[my_a]
     pl.semaphore_wait(barrier, a - 1 + b - 1)
 
-    def first(k, to, slot):
-        return remote(part_ref.at[to], got.at[slot], s_a.at[k], r_a.at[slot], id_a(to))
-
-    def second(k, to, slot):
-        return remote(mine_sum, rows.at[slot], s_b.at[k], r_b.at[slot], id_b(to))
-
-    def third(k, to, slot):
-        return remote(full.at[my_a], full.at[slot], s_c.at[k], r_c.at[slot], id_a(to))
+    def first(to, slot):
+        return remote(part_ref.at[to], got.at[slot], s_a.at[0], r_a.at[0], id_a(to))
+
+    def second(to, slot):
+        return remote(mine_sum, rows.at[slot], s_b.at[0], r_b.at[0], id_b(to))
+
+    def third(to, slot):
+        return remote(full.at[my_a], full.at[slot], s_c.at[0], r_c.at[0], id_a(to))
 
     def start(mine, count, copy):
-        each(count, lambda k: copy(k, ahead(mine, count, k), mine).start())
-
-    def arrive(mine, count, copy):
-        each(
-            count,
-            lambda k: copy(k, behind(mine, count, k), behind(mine, count, k)).wait_recv(),
-        )
-
-    def sent(mine, count, copy):
-        each(count, lambda k: copy(k, ahead(mine, count, k), mine).wait_send())
+        each(count, lambda k: copy(ahead(mine, count, k), mine).start())
+
+    in_a, in_b = pl.ds(0, a - 1), pl.ds(0, b - 1)
+    next_a = id_a(ahead(my_a, a, 1))
+    next_b = id_b(ahead(my_b, b, 1))
+    all_first = remote(part_ref.at[in_a], got.at[in_a], s_a.at[0], r_a.at[0], next_a)
+    all_second = remote(rows.at[in_b], rows.at[in_b], s_b.at[0], r_b.at[0], next_b)
+    all_third = remote(full.at[in_a], full.at[in_a], s_c.at[0], r_c.at[0], next_a)
 
     start(my_a, a, first)
-    arrive(my_a, a, first)
+    all_first.wait_recv()
     total = got[0]
     for d in range(1, a):
         total = total + got[d]
     mine_sum[...] = total
     rows[my_b] = total
     start(my_b, b, second)
-    arrive(my_b, b, second)
+    all_second.wait_recv()
     total = rows[0]
     for d in range(1, b):
         total = total + rows[d]
     full[my_a] = total
     start(my_a, a, third)
-    arrive(my_a, a, third)
+    all_third.wait_recv()
     share = full.shape[1]
     sums = jnp.concatenate([full[k // share, k % share] for k in range(TABLE_ROWS // 8)], axis=0)
     sums = sums * (1.0 / float(ROWS * n * m))
@@ -753,9 +743,9 @@
         short_ref[i] = sums[TAPS * i : TAPS * (i + 1)]
     res_ref[...] = sums[24 : 24 + MODES]
     log_ref[...] = -residue_ref[...] * decay_ref[...] * sums[40 : 40 + MODES]
-    sent(my_a, a, first)
-    sent(my_b, b, second)
-    sent(my_a, a, third)
+    all_first.wait_send()
+    all_second.wait_send()
+    all_third.wait_send()
 
 
 def total_sums(n, m, parts, decay_rate, residue):
@@ -779,13 +769,8 @@
             pltpu.VMEM((share, 8, groups), F32),
             pltpu.VMEM((b, share, 8, groups), F32),
             pltpu.VMEM((a, share, 8, groups), F32),
-            dma((a,)),
-            dma((a,)),
-            dma((b,)),
-            dma((b,)),
-            dma((a,)),
-            dma((a,)),
-        ],
+        ]
+        + [dma((1,))] * 6,
         compiler_params=pltpu.CompilerParams(
             collective_id=1, has_side_effects=True, vmem_limit_bytes=16 * 2**20
         ),

time: 94.5 us -> 91.9 us (0.972)
  Pallas kernels: 90.7 us -> 88.1 us
    pallas_call x1, Pallas kernels: 57 us -> 55 us  [local_part(): pl.pallas_call(partial(local_kernel, n), in_specs=[pl.BlockSpec(memory_sp...]
where the time goes in v5:
time: 91.9 us; the launch traced here: 91.5 us
  Pallas kernels  88.1 us (96%)
  local copies, waits for them, and re-layouts  2.67 us (3%)
    pallas_call x1, Pallas kernels, local_part(): pl.pallas_call(partial(local_kernel, n), in_specs=[pl.BlockSpec(memory_sp...  55 us
    pallas_call x1, Pallas kernels, finish(): pl.pallas_call(partial(finish_kernel, tiles), grid=(channels // block,),...  16.9 us
    pallas_call x1, Pallas kernels, total_sums(): pl.pallas_call(partial(total_kernel, n, m, nx, ny), out_shape=[jax.ShapeD...  16.2 us
    unnamed x9, local copies, waits for them, and re-layouts  2.67 us

profile of v5, /device:TPU:1, one launch (start us, length us, event | category | flops | bytes accessed | tf_op | source)
XLA Modules:
  0.0 91.5 jit_solution(13129752101172719038)
XLA Ops:
  0.6 55.0 %local.1 = (f32[56,4096]{1,0:T(8,128)}, f32[3,8,4096]{2,1,0:T(8,128)}, f32[4,8,4096]{2,1,0:T(8,128)}, f32[32,32,128]{2,1,0:T(8,128)}, f32[32,64,128]{2,1,0:T(8,1...) custom-call(bf16[3,128,4096]{2,1,0:T(8,128)(2,1)} %bitcast.6, ...), custom_call_target="tpu_custom_call" | custom-call | tf_op jit(solution)/shard_map/local/pallas_call | solution.py:415
  55.6 0.0 copy-start
  55.7 0.0 copy-start.1
  55.7 16.9 %finish.1 = (bf16[128,4096]{1,0:T(8,128)(2,1)}, bf16[3,128,4096]{2,1,0:T(8,128)(2,1)}, f32[64,256]{1,0:T(8,128)}) custom-call(bf16[3,128,4096]{2,1,0:T(8,128)(2,1)} %bitcast.7, bf16[128,4096]{1,0:T(8,128)(2,1)} %bitcast.9, f32[3,8,4096]{2,1,0:T(8,128)} %get-tuple-element.19.before_ref, f32[4,8,4096]{2,1,0:T(8,128)} %get-tuple-element.20.after_ref, ...), custom_call_target="tpu_custom_call" | custom-call | tf_op jit(solution)/shard_map/finish/pallas_call | solution.py:625
  72.6 0.0 copy-done
  72.6 0.0 copy-done.1
  72.6 0.0 copy-start.2
  72.6 0.8 copy-done.2
  73.4 16.2 %totals.1 = (f32[3,7,256]{2,1,0:T(8,128)S(1)}, f32[16,256]{1,0:T(8,128)S(1)}, f32[16,256]{1,0:T(8,128)S(1)}) custom-call(f32[8,1,8,256]{3,2,1,0:T(8,128)S(1)} %bitcast.5, f32[16,256]{1,0:T(8,128)S(1)} %copy-done, f32[16,256]{1,0:T(8,128)S(1)} %copy-done.1), custom_call_target="tpu_custom_call" | custom-call | tf_op jit(solution)/shard_map/totals/pallas_call | solution.py:758
  89.7 0.6 copy.13
  90.3 0.6 copy.14
  90.9 0.6 copy.15
Async XLA Ops:
  55.6 16.9 %copy-start = (f32[16,256]{1,0:T(8,128)S(1)}, f32[16,256]{1,0:T(8,128)}, u32[]{:S(2)}) copy-start(f32[16,256]{1,0:T(8,128)} %decay_ref.3) | copy-start | bytes 49156
  55.7 16.9 %copy-start.1 = (f32[16,256]{1,0:T(8,128)S(1)}, f32[16,256]{1,0:T(8,128)}, u32[]{:S(2)}) copy-start(f32[16,256]{1,0:T(8,128)} %residue_ref.3) | copy-start | bytes 49156
  72.6 0.8 copy-start.2

commit v6 on v5

--- a/solution.py
+++ b/solution.py
@@ -40,10 +40,6 @@
 
 def in_group(rows, width, group):
     return (iota((rows, width), 1) % LANES) // GROUP == group
-
-
-def flip_matrix():
-    return (iota((ROWS, ROWS), 0) + iota((ROWS, ROWS), 1) == ROWS - 1).astype(BF16)
 
 
 def load_tokens(pad, proj_ref, before_ref, lanes):
@@ -243,10 +239,20 @@
                 if start < HALF:
                     begin = begin + HALF
                     rights[way][begin : begin + step, 2 * LANES : 3 * LANES] = value
-            high, low = split(cot_ref[rows, lanes].astype(F32) * f[0])
+            value = cot_ref[rows, lanes].astype(F32) * f[0]
+            turn = 7 - iota((8, LANES), 0)
+            turned = jnp.concatenate(
+                [
+                    jnp.take_along_axis(value[r : r + 8], turn, axis=0)
+                    for r in range(step - 8, -8, -8)
+                ],
+                axis=0,
+            )
+            high, low = split(turned)
             begin = 2 * LANES * way
-            parts[rows, begin : begin + LANES] = high
-            parts[rows, begin + LANES : begin + 2 * LANES] = low
+            at = slice(ROWS - step - start, ROWS - start)
+            parts[at, begin : begin + LANES] = high
+            parts[at, begin + LANES : begin + 2 * LANES] = low
 
     def place(tile, way, flipped):
         streams[tile, :, 2 * LANES : 4 * LANES] = flipped
@@ -267,9 +273,8 @@
         ks = [step * GROUPED + way for way in range(GROUPED)]
         for way, k in enumerate(ks):
             features(peer_of(k), way)
-        flipped = dot(flip_matrix(), parts[...]).astype(BF16)
         for way, k in enumerate(ks):
-            place(peer_of(k), way, flipped[:, 2 * LANES * way : 2 * LANES * (way + 1)])
+            place(peer_of(k), way, parts[:, 2 * LANES * way : 2 * LANES * (way + 1)])
         for way, k in enumerate(ks):
             tile = peer_of(k)
             products[way][...] = dot(tables[tile], rights[way][:, 0 : 2 * LANES])

time: 91.9 us -> 90.9 us (0.989)
  Pallas kernels: 88.1 us -> 87.1 us
    pallas_call x1, Pallas kernels: 55 us -> 54 us  [local_part(): pl.pallas_call(partial(local_kernel, n), in_specs=[pl.BlockSpec(memory_sp...]
where the time goes in v6:
time: 90.9 us; the launch traced here: 90.4 us
  Pallas kernels  87.1 us (96%)
  local copies, waits for them, and re-layouts  2.67 us (3%)
    pallas_call x1, Pallas kernels, local_part(): pl.pallas_call(partial(local_kernel, n), in_specs=[pl.BlockSpec(memory_sp...  54 us
    pallas_call x1, Pallas kernels, finish(): pl.pallas_call(partial(finish_kernel, tiles), grid=(channels // block,),...  16.9 us
    pallas_call x1, Pallas kernels, total_sums(): pl.pallas_call(partial(total_kernel, n, m, nx, ny), out_shape=[jax.ShapeD...  16.2 us
    unnamed x9, local copies, waits for them, and re-layouts  2.67 us

profile of v6, /device:TPU:1, one launch (start us, length us, event | category | flops | bytes accessed | tf_op | source)
XLA Modules:
  0.0 90.4 jit_solution(11525861486335291895)
XLA Ops:
  0.6 54.0 %local.1 = (f32[56,4096]{1,0:T(8,128)}, f32[3,8,4096]{2,1,0:T(8,128)}, f32[4,8,4096]{2,1,0:T(8,128)}, f32[32,32,128]{2,1,0:T(8,128)}, f32[32,64,128]{2,1,0:T(8,1...) custom-call(bf16[3,128,4096]{2,1,0:T(8,128)(2,1)} %bitcast.6, ...), custom_call_target="tpu_custom_call" | custom-call | tf_op jit(solution)/shard_map/local/pallas_call | solution.py:420
  54.6 0.0 copy-start
  54.6 0.0 copy-start.1
  54.6 16.9 %finish.1 = (bf16[128,4096]{1,0:T(8,128)(2,1)}, bf16[3,128,4096]{2,1,0:T(8,128)(2,1)}, f32[64,256]{1,0:T(8,128)}) custom-call(bf16[3,128,4096]{2,1,0:T(8,128)(2,1)} %bitcast.7, bf16[128,4096]{1,0:T(8,128)(2,1)} %bitcast.9, f32[3,8,4096]{2,1,0:T(8,128)} %get-tuple-element.19.before_ref, f32[4,8,4096]{2,1,0:T(8,128)} %get-tuple-element.20.after_ref, ...), custom_call_target="tpu_custom_call" | custom-call | tf_op jit(solution)/shard_map/finish/pallas_call | solution.py:630
  71.5 0.0 copy-done
  71.5 0.0 copy-done.1
  71.6 0.0 copy-start.2
  71.6 0.8 copy-done.2
  72.4 16.2 %totals.1 = (f32[3,7,256]{2,1,0:T(8,128)S(1)}, f32[16,256]{1,0:T(8,128)S(1)}, f32[16,256]{1,0:T(8,128)S(1)}) custom-call(f32[8,1,8,256]{3,2,1,0:T(8,128)S(1)} %bitcast.5, f32[16,256]{1,0:T(8,128)S(1)} %copy-done, f32[16,256]{1,0:T(8,128)S(1)} %copy-done.1), custom_call_target="tpu_custom_call" | custom-call | tf_op jit(solution)/shard_map/totals/pallas_call | solution.py:763
  88.6 0.6 copy.13
  89.2 0.6 copy.14
  89.8 0.6 copy.15
Async XLA Ops:
  54.6 16.9 %copy-start = (f32[16,256]{1,0:T(8,128)S(1)}, f32[16,256]{1,0:T(8,128)}, u32[]{:S(2)}) copy-start(f32[16,256]{1,0:T(8,128)} %decay_ref.3) | copy-start | bytes 49156
  54.6 16.9 %copy-start.1 = (f32[16,256]{1,0:T(8,128)S(1)}, f32[16,256]{1,0:T(8,128)}, u32[]{:S(2)}) copy-start(f32[16,256]{1,0:T(8,128)} %residue_ref.3) | copy-start | bytes 49156
  71.6 0.8 copy-start.2

commit v7 on v6

--- a/solution.py
+++ b/solution.py
@@ -198,7 +198,10 @@
                 store_table(tile, slice(begin, begin + MODES), value)
         return carry
 
-    lax.fori_loop(0, n, build_tables, 0)
+    def build_two(step, carry):
+        return build_tables(2 * step + 1, build_tables(2 * step, carry))
+
+    lax.fori_loop(0, n // 2, build_two, 0)
     for way in range(GROUPED):
         for k in range(3):
             begin = ROWS * k

time: 90.9 us -> 89.5 us (0.985)
  Pallas kernels: 87.1 us -> 85.7 us
    pallas_call x1, Pallas kernels: 54 us -> 51.9 us  [local_part(): pl.pallas_call(partial(local_kernel, n), in_specs=[pl.BlockSpec(memory_sp...]
where the time goes in v7:
time: 89.5 us; the launch traced here: 89 us
  Pallas kernels  85.7 us (96%)
  local copies, waits for them, and re-layouts  2.67 us (3%)
    pallas_call x1, Pallas kernels, local_part(): pl.pallas_call(partial(local_kernel, n), in_specs=[pl.BlockSpec(memory_sp...  51.9 us
    pallas_call x1, Pallas kernels, finish(): pl.pallas_call(partial(finish_kernel, tiles), grid=(channels // block,),...  16.9 us
    pallas_call x1, Pallas kernels, total_sums(): pl.pallas_call(partial(total_kernel, n, m, nx, ny), out_shape=[jax.ShapeD...  16.9 us
    unnamed x9, local copies, waits for them, and re-layouts  2.67 us

profile of v7, /device:TPU:1, one launch (start us, length us, event | category | flops | bytes accessed | tf_op | source)
XLA Modules:
  0.0 89.0 jit_solution(15854049569383724549)
XLA Ops:
  0.6 51.9 %local.1 = (f32[56,4096]{1,0:T(8,128)}, f32[3,8,4096]{2,1,0:T(8,128)}, f32[4,8,4096]{2,1,0:T(8,128)}, f32[32,32,128]{2,1,0:T(8,128)}, f32[32,64,128]{2,1,0:T(8,1...) custom-call(bf16[3,128,4096]{2,1,0:T(8,128)(2,1)} %bitcast.6, ...), custom_call_target="tpu_custom_call" | custom-call | tf_op jit(solution)/shard_map/local/pallas_call | solution.py:423
  52.5 0.0 copy-start
  52.5 0.0 copy-start.1
  52.6 16.9 %finish.1 = (bf16[128,4096]{1,0:T(8,128)(2,1)}, bf16[3,128,4096]{2,1,0:T(8,128)(2,1)}, f32[64,256]{1,0:T(8,128)}) custom-call(bf16[3,128,4096]{2,1,0:T(8,128)(2,1)} %bitcast.7, bf16[128,4096]{1,0:T(8,128)(2,1)} %bitcast.9, f32[3,8,4096]{2,1,0:T(8,128)} %get-tuple-element.19.before_ref, f32[4,8,4096]{2,1,0:T(8,128)} %get-tuple-element.20.after_ref, ...), custom_call_target="tpu_custom_call" | custom-call | tf_op jit(solution)/shard_map/finish/pallas_call | solution.py:633
  69.5 0.0 copy-done
  69.5 0.0 copy-done.1
  69.5 0.0 copy-start.2
  69.5 0.8 copy-done.2
  70.3 16.9 %totals.1 = (f32[3,7,256]{2,1,0:T(8,128)S(1)}, f32[16,256]{1,0:T(8,128)S(1)}, f32[16,256]{1,0:T(8,128)S(1)}) custom-call(f32[8,1,8,256]{3,2,1,0:T(8,128)S(1)} %bitcast.5, f32[16,256]{1,0:T(8,128)S(1)} %copy-done, f32[16,256]{1,0:T(8,128)S(1)} %copy-done.1), custom_call_target="tpu_custom_call" | custom-call | tf_op jit(solution)/shard_map/totals/pallas_call | solution.py:766
  87.2 0.6 copy.13
  87.8 0.6 copy.14
  88.4 0.6 copy.15
Async XLA Ops:
  52.5 16.9 %copy-start = (f32[16,256]{1,0:T(8,128)S(1)}, f32[16,256]{1,0:T(8,128)}, u32[]{:S(2)}) copy-start(f32[16,256]{1,0:T(8,128)} %decay_ref.3) | copy-start | bytes 49156
  52.5 16.9 %copy-start.1 = (f32[16,256]{1,0:T(8,128)S(1)}, f32[16,256]{1,0:T(8,128)}, u32[]{:S(2)}) copy-start(f32[16,256]{1,0:T(8,128)} %residue_ref.3) | copy-start | bytes 49156
  69.5 0.8 copy-start.2
